TPU v7x, 32 devices: a whole 2x2x4 slice. The times are simulated.
32 devices in a mesh: dp: 8 (over z, y), map: 4 (over x, core).
Axes of the slice: x: 2, y: 2, z: 4, core: 2. Of those that a mesh axis runs over, the one named last changes fastest.
Arguments:
- embeddings: bfloat16 [32768, 256], P('dp'), may hold values from -96 to 96
- winners: int32 [32768], P('dp'), may hold values from 0 to 65535, as said below
- codebook: float32 [256, 256, 256], P('dp', 'map'), may hold values from -6 to 6
Outputs:
- updated: float32 [256, 256, 256], P('dp', 'map')
- updated_copy: bfloat16 [256, 256, 256], P('dp', 'map')
Inputs may be any that keep to these rules, and one draw needn't show every extreme that they name: `winners`: the winning node of each row, numbered c * 256 + r for map column c and map row r; within the rows of one index of dp (aligned blocks of 4096 rows), at most 256 rows win a node of any one tile of 256 / 8 map columns by 256 / 4 map rows (tile of columns c // (256 / 8) and rows r // (256 / 4)), and in every block some tile has exactly 256.
All inputs are finite; a program needn't handle non-finite values.
Results may differ from a plain program's by a relative error of at most 0.0075.
Values may be sent and summed in bfloat16 or wider, within the bound.
A program may use at most 64 MiB of HBM per device.

v0:
```python
import jax
import jax.numpy as jnp
from jax import lax
from jax.sharding import PartitionSpec as P

REACH = 16


def extended_2(cells, sides, width):
    for axis, dim in sides:
        count = lax.axis_size(axis)
        ends = count - 1
        head = lax.slice_in_dim(cells, 0, width, axis=dim)
        tail = lax.slice_in_dim(cells, cells.shape[dim] - width, cells.shape[dim], axis=dim)
        cells = jnp.concatenate(
            [
                lax.ppermute(tail, axis, [(i, (i + 1) % count) for i in range(ends)]),
                cells,
                lax.ppermute(head, axis, [((i + 1) % count, i) for i in range(ends)]),
            ],
            axis=dim,
        )
    return cells


def band_weights(count, reach, sigma):
    local = jnp.arange(count, dtype=jnp.int32)
    extended = jnp.arange(count + 2 * reach, dtype=jnp.int32)
    gap = local[:, None] - extended[None, :] + reach
    apart = gap.astype(jnp.float32) / sigma
    return jnp.where(jnp.abs(gap) <= reach, jnp.exp(-0.5 * apart * apart) / sigma, 0.0)


def smooth_columns(extended, weights):
    highest = lax.Precision.HIGHEST
    ext_num, ext_den = extended
    return (
        jnp.einsum("aj,jre->are", weights, ext_num, precision=highest),
        jnp.dot(weights, ext_den, precision=highest),
    )


def on_device(embeddings, winners, codebook):
    highest = lax.Precision.HIGHEST
    cols_local, band, width = codebook.shape
    n_dp = lax.axis_size("dp")
    n_map = lax.axis_size("map")
    map_rows = band * n_map
    sigma = float(REACH) / 2.0
    first_row = lax.axis_index("map") * band
    column = winners // map_rows
    row_of = winners - column * map_rows
    inside = (row_of >= first_row) & (row_of < first_row + band)
    column_weights = band_weights(cols_local, REACH, sigma)
    row_weights = band_weights(band, REACH, sigma)
    rows_dev = embeddings.shape[0]
    capacity = max(2, 2 * rows_dev // (n_dp * n_map))
    target = column // cols_local
    hits = (
        (target[:, None] == jnp.arange(n_dp, dtype=jnp.int32)[None, :]) & inside[:, None]
    ).astype(jnp.int32)
    slot = jnp.sum((jnp.cumsum(hits, axis=0) - 1) * hits, axis=1)
    position = jnp.where(inside, target * capacity + slot, n_dp * capacity)
    tile_key = (column - target * cols_local) * band + row_of - first_row
    outgoing = jnp.zeros((n_dp * capacity + 1, width), jnp.bfloat16).at[position].set(embeddings)
    out_keys = jnp.full((n_dp * capacity + 1,), -1, jnp.int32).at[position].set(tile_key)
    outgoing = outgoing[: n_dp * capacity].reshape(n_dp, capacity, width)
    out_keys = out_keys[: n_dp * capacity].reshape(n_dp, capacity)
    incoming, in_keys = (
        lax.all_to_all(outgoing, "dp", split_axis=0, concat_axis=0, tiled=True),
        lax.all_to_all(out_keys, "dp", split_axis=0, concat_axis=0, tiled=True),
    )
    incoming = incoming.reshape(n_dp * capacity, width)
    in_keys = in_keys.reshape(n_dp * capacity)
    tile_nodes = cols_local * band
    onehot = (in_keys[:, None] == jnp.arange(tile_nodes, dtype=jnp.int32)[None, :]).astype(
        jnp.bfloat16
    )
    tile_sum = lax.dot_general(
        onehot, incoming, (((0,), (0,)), ((), ())), preferred_element_type=jnp.float32
    )
    tile_count = jnp.sum(onehot, axis=0, dtype=jnp.float32)
    tile_num = tile_sum.reshape(cols_local, band, width)
    tile_den = tile_count.reshape(cols_local, band)
    extended = (
        extended_2(tile_num, (("dp", 0),), REACH),
        extended_2(tile_den, (("dp", 0),), REACH),
    )
    tile_num, tile_den = smooth_columns(extended, column_weights)
    ext_num, ext_den = (
        extended_2(tile_num, (("map", 1),), REACH),
        extended_2(tile_den, (("map", 1),), REACH),
    )
    num = jnp.einsum("bj,cje->cbe", row_weights, ext_num, precision=highest)
    den = jnp.einsum("bj,cj->cb", row_weights, ext_den, precision=highest)
    updated = 0.1 * codebook + 0.9 * (num + codebook) / (den[:, :, None] + 1.0)
    return (updated, updated.astype(jnp.bfloat16))


def solution(mesh):
    placed = (P("dp", None), P("dp"), P("dp", "map", None))
    return jax.shard_map(
        on_device,
        mesh=mesh,
        in_specs=placed,
        out_specs=(P("dp", "map", None), P("dp", "map", None)),
        check_vma=False,
    )
```

profile of v0, /device:TPU:1, one launch (start us, length us, event | category | flops | bytes accessed | tf_op | source)
XLA Modules:
  0.0 166.8 jit_solution(3218926998189581281)
XLA Ops:
  0.6 0.7 fusion.85
  1.4 0.7 compare_and_fusion
  2.1 0.8 add_subtract_fusion
  2.9 2.3 %reduce-window.6 = s32[8,32,128]{2,1,0:T(8,128)S(1)} reduce-window(s32[8,32,128]{2,1,0:T(8,128)S(1)} %fusion.20, s32[]{:T(128)} %constant.62.clone.1), window={size=1x1x128 pad=0_0x0_0x127_0}, to_apply=%region_0.1 | reduce-window | flops 4161536 | bytes 262148 | tf_op jit(solution)/shard_map/reduce-window
  5.2 0.3 slice_reduce_fusion
  6.0 0.7 compare_select_fusion
  6.7 15.5 %scatter_custom_fusion = s32[2049]{0:T(1024)S(1)} fusion(s32[4096]{0:T(1024)S(1)} %compare_select_fusion, s32[4096]{0:T(1024)S(1)} %get-tuple-element.2, s32[]{:T(128)} %constant.60.clone.1), kind=kCustom, calls=%fused_computation.84 | custom fusion | bytes 8200 | tf_op jit(solution)/shard_map/scatter | solution.py:66
  22.2 0.6 slice.81
  22.8 6.4 %all-to-all-start = ((s32[8,1,256]{2,1,0:T(1,128)}), s32[8,1,256]{2,1,0:T(1,128)S(1)}, u32[]{:S(2)}, u32[]{:S(2)}) async-start(s32[8,1,256]{2,1,0:T(1,128)} %bitcast.4), calls=%async_computation | async-start | bytes 16384 | tf_op jit(solution)/shard_map/all_to_all | solution.py:71
  29.2 18.4 %scatter_custom_fusion.1 = bf16[2049,256]{1,0:T(8,128)(2,1)S(1)} fusion(s32[4096]{0:T(1024)S(1)} %compare_select_fusion, bf16[4096,256]{1,0:T(8,128)(2,1)} %param.3, bf16[]{:T(256)} %constant.73.clone.1), kind=kCustom, calls=%fused_computation.21 | custom fusion | bytes 1049600 | tf_op jit(solution)/shard_map/scatter | solution.py:65
  47.7 30.0 %all_to_all.14 = bf16[8,256,256]{2,1,0:T(8,128)(2,1)S(1)} all-to-all(bf16[8,256,256]{2,1,0:T(8,128)(2,1)S(1)} %bitcast.47), channel_id=1, replica_groups=mesh['dp'=8,'map'=4] {'dp'}, dimensions={0} | all-to-all | bytes 2097152 | tf_op jit(solution)/shard_map/all_to_all | solution.py:70
  77.7 4.9 %fusion.1 = f32[2048,256]{1,0:T(8,128)S(1)} fusion(bf16[2048,256]{1,0:T(8,128)(2,1)S(1)} %bitcast.50, s32[2048]{0:T(1024)S(1)} %bitcast.53), kind=kOutput, calls=%fused_computation.5 | convolution fusion | flops 2151677952 | bytes 3153920 | tf_op jit(solution)/shard_map/dot_general | solution.py:79
  82.8 0.6 copy.13
  83.4 0.6 copy.14
  84.1 1.3 collective-permute-start.1
  85.4 4.2 %collective-permute-start = (f32[16,64,256]{2,0,1:T(8,128)S(1)}, f32[16,64,256]{2,0,1:T(8,128)S(1)}, u32[]{:S(2)}, u32[]{:S(2)}) collective-permute-start(f32[16,64,256]{2,0,1:T(8,128)S(1)} %copy.13), channel_id=1, source_target_pairs={{0,4},{4,8},{8,12},{12,16},{16,20},{20,24},{24,28},{1,5},{5,9},{9,... | collective-permute-start | bytes 3145736 | tf_op jit(solution)/shard_map/ppermute | solution.py:17
  89.6 2.1 %convert_reduce_fusion = f32[2048]{0:T(1024)S(1)} fusion(s32[2048]{0:T(1024)S(1)} %bitcast.54), kind=kLoop, calls=%fused_computation.2 | loop fusion | flops 16775168 | bytes 16384 | tf_op jit(solution)/shard_map/reduce_sum | solution.py:82
  91.7 1.2 copy.15
  92.9 15.7 %collective-permute-done.1 = f32[16,64,256]{2,0,1:T(8,128)S(1)} collective-permute-done((f32[16,64,256]{2,0,1:T(8,128)S(1)}, f32[16,64,256]{2,0,1:T(8,128)S(1)}, u32[]{:S(2)}, u32[]{:S(2)}) %collective-permute-start.1) | collective-permute-done | bytes 1048608 | tf_op jit(solution)/shard_map/ppermute | solution.py:19
  108.6 24.9 %collective-permute-done = f32[16,64,256]{2,0,1:T(8,128)S(1)} collective-permute-done((f32[16,64,256]{2,0,1:T(8,128)S(1)}, f32[16,64,256]{2,0,1:T(8,128)S(1)}, u32[]{:S(2)}, u32[]{:S(2)}) %collective-permute-start) | collective-permute-done | bytes 1048608 | tf_op jit(solution)/shard_map/ppermute | solution.py:17
  133.5 2.1 %fusion.3 = f32[32,64,256]{2,0,1:T(8,128)S(1)} fusion(f32[16,64,256]{2,0,1:T(8,128)S(1)} %collective-permute-done.1, f32[32,64,256]{2,0,1:T(8,128)S(1)} %copy.15, f32[16,64,256]{2,0,1:T(8,128)S(1)} %collective-permute-done), kind=kOutput, calls=%fused_computation.7 | convolution fusion | flops 404770816 | bytes 6291456 | tf_op jit(solution)/shard_map/aj,jre->are/dot_general | solution.py:38
  135.6 1.0 fusion.79
  136.6 3.5 %collective-permute-start.2 = (f32[32,16,256]{2,0,1:T(8,128)}, f32[32,16,256]{2,0,1:T(8,128)S(1)}, u32[]{:S(2)}, u32[]{:S(2)}) collective-permute-start(f32[32,16,256]{2,0,1:T(8,128)} %get-tuple-element.4), channel_id=1, source_target_pairs={{0,1},{1,2},{2,3},{4,5},{5,6},{6,7},{8,9},{9,10},{10,11},{12,13},{... | collective-permute-start | bytes 1572872 | tf_op jit(solution)/shard_map/ppermute | solution.py:17
  140.1 1.9 %collective-permute-start.3 = (f32[32,16,256]{2,0,1:T(8,128)}, f32[32,16,256]{2,0,1:T(8,128)S(1)}, u32[]{:S(2)}, u32[]{:S(2)}) collective-permute-start(f32[32,16,256]{2,0,1:T(8,128)} %get-tuple-element.5), channel_id=1, source_target_pairs={{1,0},{2,1},{3,2},{5,4},{6,5},{7,6},{9,8},{10,9},{11,10},{13,12},{... | collective-permute-start | bytes 1572872 | tf_op jit(solution)/shard_map/ppermute | solution.py:19
  142.2 1.3 collective-permute-start.5
  143.5 4.7 %collective-permute-start.4 = (f32[16,64]{1,0:T(8,128)S(1)}, f32[16,64]{1,0:T(8,128)S(1)}, u32[]{:S(2)}, u32[]{:S(2)}) collective-permute-start(f32[16,64]{1,0:T(8,128)S(1)} %slice.75), channel_id=1, source_target_pairs={{0,4},{4,8},{8,12},{12,16},{16,20},{20,24},{24,28},{1,5},{5,9},{9,... | collective-permute-start | bytes 12296 | tf_op jit(solution)/shard_map/ppermute | solution.py:17
  148.3 0.7 collective-permute-done.4
  149.2 4.5 %collective-permute-start.6 = (f32[32,16]{1,0:T(8,128)S(1)}, f32[32,16]{1,0:T(8,128)S(1)}, u32[]{:S(2)}, u32[]{:S(2)}) collective-permute-start(f32[32,16]{1,0:T(8,128)S(1)} %get-tuple-element.8), channel_id=1, source_target_pairs={{0,1},{1,2},{2,3},{4,5},{5,6},{6,7},{8,9},{9,10},{10,11},{12,13},{... | collective-permute-start | bytes 6152 | tf_op jit(solution)/shard_map/ppermute | solution.py:17
  153.7 1.9 %collective-permute-start.7 = (f32[32,16]{1,0:T(8,128)S(1)}, f32[32,16]{1,0:T(8,128)S(1)}, u32[]{:S(2)}, u32[]{:S(2)}) collective-permute-start(f32[32,16]{1,0:T(8,128)S(1)} %get-tuple-element.9), channel_id=1, source_target_pairs={{1,0},{2,1},{3,2},{5,4},{6,5},{7,6},{9,8},{10,9},{11,10},{13,12},{... | collective-permute-start | bytes 6152 | tf_op jit(solution)/shard_map/ppermute | solution.py:19
  155.7 3.1 %collective-permute-done.7 = f32[32,16]{1,0:T(8,128)S(1)} collective-permute-done((f32[32,16]{1,0:T(8,128)S(1)}, f32[32,16]{1,0:T(8,128)S(1)}, u32[]{:S(2)}, u32[]{:S(2)}) %collective-permute-start.7) | collective-permute-done | bytes 2080 | tf_op jit(solution)/shard_map/ppermute | solution.py:19
  159.3 1.3 copy-done
  160.6 6.2 %fusion.83 = (bf16[32,64,256]{2,1,0:T(8,128)(2,1)}, f32[32,64,256]{2,1,0:T(8,128)}) fusion(f32[32,64]{1,0:T(8,128)S(1)} %convolution_add_fusion, f32[32,64,256]{2,1,0:T(8,128)S(1)} %copy-done, f32[32,96,256]{2,0,1:T(8,128)S(1)} %pad_maximum_fusion), kind=kOutput, calls=%fused_computation.109 | convolution fusion | flops 607186944 | bytes 8396800 | tf_op jit(solution)/shard_map/bj,cje->cbe/dot_general | solution.py:94
  (20 shorter events, 1.6 us)
Async XLA Ops:
  22.8 24.9 %all-to-all-start = ((s32[8,1,256]{2,1,0:T(1,128)}), s32[8,1,256]{2,1,0:T(1,128)S(1)}, u32[]{:S(2)}, u32[]{:S(2)}) async-start(s32[8,1,256]{2,1,0:T(1,128)} %bitcast.4), calls=%async_computation | async-start | bytes 16384 | tf_op jit(solution)/shard_map/all_to_all | solution.py:71
  84.1 24.5 %collective-permute-start.1 = (f32[16,64,256]{2,0,1:T(8,128)S(1)}, f32[16,64,256]{2,0,1:T(8,128)S(1)}, u32[]{:S(2)}, u32[]{:S(2)}) collective-permute-start(f32[16,64,256]{2,0,1:T(8,128)S(1)} %copy.14), channel_id=1, source_target_pairs={{4,0},{8,4},{12,8},{16,12},{20,16},{24,20},{28,24},{5,1},{9,5},{13... | collective-permute-start | bytes 3145736 | tf_op jit(solution)/shard_map/ppermute | solution.py:19
  85.4 48.1 %collective-permute-start = (f32[16,64,256]{2,0,1:T(8,128)S(1)}, f32[16,64,256]{2,0,1:T(8,128)S(1)}, u32[]{:S(2)}, u32[]{:S(2)}) collective-permute-start(f32[16,64,256]{2,0,1:T(8,128)S(1)} %copy.13), channel_id=1, source_target_pairs={{0,4},{4,8},{8,12},{12,16},{16,20},{20,24},{24,28},{1,5},{5,9},{9,... | collective-permute-start | bytes 3145736 | tf_op jit(solution)/shard_map/ppermute | solution.py:17
  136.6 22.4 %collective-permute-start.2 = (f32[32,16,256]{2,0,1:T(8,128)}, f32[32,16,256]{2,0,1:T(8,128)S(1)}, u32[]{:S(2)}, u32[]{:S(2)}) collective-permute-start(f32[32,16,256]{2,0,1:T(8,128)} %get-tuple-element.4), channel_id=1, source_target_pairs={{0,1},{1,2},{2,3},{4,5},{5,6},{6,7},{8,9},{9,10},{10,11},{12,13},{... | collective-permute-start | bytes 1572872 | tf_op jit(solution)/shard_map/ppermute | solution.py:17
  140.1 18.9 %collective-permute-start.3 = (f32[32,16,256]{2,0,1:T(8,128)}, f32[32,16,256]{2,0,1:T(8,128)S(1)}, u32[]{:S(2)}, u32[]{:S(2)}) collective-permute-start(f32[32,16,256]{2,0,1:T(8,128)} %get-tuple-element.5), channel_id=1, source_target_pairs={{1,0},{2,1},{3,2},{5,4},{6,5},{7,6},{9,8},{10,9},{11,10},{13,12},{... | collective-permute-start | bytes 1572872 | tf_op jit(solution)/shard_map/ppermute | solution.py:19
  142.2 6.1 %collective-permute-start.5 = (f32[16,64]{1,0:T(8,128)S(1)}, f32[16,64]{1,0:T(8,128)S(1)}, u32[]{:S(2)}, u32[]{:S(2)}) collective-permute-start(f32[16,64]{1,0:T(8,128)S(1)} %slice.77), channel_id=1, source_target_pairs={{4,0},{8,4},{12,8},{16,12},{20,16},{24,20},{28,24},{5,1},{9,5},{13... | collective-permute-start | bytes 12296 | tf_op jit(solution)/shard_map/ppermute | solution.py:19
  143.5 5.5 %collective-permute-start.4 = (f32[16,64]{1,0:T(8,128)S(1)}, f32[16,64]{1,0:T(8,128)S(1)}, u32[]{:S(2)}, u32[]{:S(2)}) collective-permute-start(f32[16,64]{1,0:T(8,128)S(1)} %slice.75), channel_id=1, source_target_pairs={{0,4},{4,8},{8,12},{12,16},{16,20},{20,24},{24,28},{1,5},{5,9},{9,... | collective-permute-start | bytes 12296 | tf_op jit(solution)/shard_map/ppermute | solution.py:17
  149.2 6.4 %collective-permute-start.6 = (f32[32,16]{1,0:T(8,128)S(1)}, f32[32,16]{1,0:T(8,128)S(1)}, u32[]{:S(2)}, u32[]{:S(2)}) collective-permute-start(f32[32,16]{1,0:T(8,128)S(1)} %get-tuple-element.8), channel_id=1, source_target_pairs={{0,1},{1,2},{2,3},{4,5},{5,6},{6,7},{8,9},{9,10},{10,11},{12,13},{... | collective-permute-start | bytes 6152 | tf_op jit(solution)/shard_map/ppermute | solution.py:17
  153.7 5.1 %collective-permute-start.7 = (f32[32,16]{1,0:T(8,128)S(1)}, f32[32,16]{1,0:T(8,128)S(1)}, u32[]{:S(2)}, u32[]{:S(2)}) collective-permute-start(f32[32,16]{1,0:T(8,128)S(1)} %get-tuple-element.9), channel_id=1, source_target_pairs={{1,0},{2,1},{3,2},{5,4},{6,5},{7,6},{9,8},{10,9},{11,10},{13,12},{... | collective-permute-start | bytes 6152 | tf_op jit(solution)/shard_map/ppermute | solution.py:19
  159.0 1.6 copy-start
where the time goes:
time: 170 us; the launch traced here: 167 us
  waiting for transfers between devices  44.4 us (26%)
  local copies, waits for them, and re-layouts  40.2 us (24%)
  blocking collectives  30 us (18%)
  starting transfers between devices  29.7 us (17%)
  matrix products  13.6 us (8%)
  other arithmetic  8.03 us (5%)
    all_to_all x1, blocking collectives, on_device(): lax.all_to_all(outgoing, 'dp', split_axis=0, concat_axis=0, tiled=True)  30 us
    ppermute x4, waiting for transfers between devices, extended_2(): lax.ppermute(tail, axis, [(i, (i + 1) % count) for i in range(ends)])  25.6 us
    ppermute x4, waiting for transfers between devices, extended_2(): lax.ppermute(head, axis, [((i + 1) % count, i) for i in range(ends)])  18.8 us
    scatter x1, local copies, waits for them, and re-layouts, on_device(): jnp.zeros((n_dp * capacity + 1, width), jnp.bfloat16).at[position]  18.4 us
    ppermute x4, starting transfers between devices, extended_2(): lax.ppermute(tail, axis, [(i, (i + 1) % count) for i in range(ends)])  16.9 us
    scatter x1, local copies, waits for them, and re-layouts, on_device(): jnp.full((n_dp * capacity + 1,), -1, jnp.int32).at[position].set(tile_key)  15.5 us
    ppermute x4, starting transfers between devices, extended_2(): lax.ppermute(head, axis, [((i + 1) % count, i) for i in range(ends)])  6.41 us
    all_to_all x1, starting transfers between devices, on_device(): lax.all_to_all(out_keys, 'dp', split_axis=0, concat_axis=0, tiled=True)  6.38 us
  transfers between devices with their start and end apart: 9, of which 4 were waited for; matrix products, arithmetic and copies ran while one was open for 13% of the time, Pallas kernels for 0%

commit v1 on v0

v1 whole, which is shorter than its diff:
```python
import functools

import jax
import jax.numpy as jnp
from jax import lax
from jax.experimental import pallas as pl
from jax.experimental.pallas import tpu as pltpu
from jax.sharding import PartitionSpec as P

REACH = 16
SIGMA = float(REACH) / 2.0
PARTS = 2
MESH = pl.DeviceIdType.MESH
NT = (((1,), (1,)), ((), ()))


def iota(shape, dim):
    return lax.broadcasted_iota(jnp.int32, shape, dim)


def over(values, size):
    if size & (size - 1) == 0:
        return lax.shift_right_logical(values, jnp.int32(size.bit_length() - 1))
    return values // size


def weight(gap):
    apart = gap / SIGMA
    return jnp.where(jnp.abs(gap) <= REACH, jnp.exp(-0.5 * apart * apart) / SIGMA, 0.0)


def exchange_kernel(
    dims, emb_ref, win_ref, ext_ref, den_ref,
    rank, tags, x_out, x_in, k_out, k_in, cw, rm, mix, own, h_out, h_in, d_out, d_in, d_own, t1, m_in, dm_in,
    x_ss, x_rs, k_ss, k_rs, h_ss, h_rs, d_ss, d_rs, m_ss, m_rs, dm_ss, dm_rs,
):
    n_dp, n_map, cap, cols, band, rows, width = dims
    part = width // PARTS
    slots = n_dp * cap
    edge = REACH * band
    me = lax.axis_index("dp")
    mm = lax.axis_index("map")
    left, right = lax.rem(me + n_dp - 1, n_dp), lax.rem(me + 1, n_dp)
    up, down = lax.rem(mm + n_map - 1, n_map), lax.rem(mm + 1, n_map)

    barrier = pltpu.get_barrier_semaphore()
    for k in range(1, n_dp):
        pl.semaphore_signal(
            barrier, inc=1, device_id=(lax.rem(me + k, n_dp), mm), device_id_type=MESH
        )
    for other in (up, down):
        pl.semaphore_signal(barrier, inc=1, device_id=(me, other), device_id_type=MESH)

    win = win_ref[...]
    column = over(win, band * n_map)
    row_of = win - column * (band * n_map) - mm * band
    target = over(column, cols)
    local = column - target * cols
    inside = (row_of >= 0) & (row_of < band)
    target = jnp.where(inside, target, -1)
    which = iota((16, rows), 0)
    tags[...] = jnp.where(
        which == 0,
        local.astype(jnp.float32),
        jnp.where(which == 1, row_of.astype(jnp.float32), jnp.where(which == 2, 1.0, 0.0)),
    ).astype(jnp.bfloat16)
    step = 256
    upper = jnp.where(iota((step, step), 0) <= iota((step, step), 1), 1.0, 0.0).astype(jnp.bfloat16)
    hits = jnp.where(target == iota((n_dp, rows), 0), 1.0, 0.0)
    carry = jnp.zeros((n_dp, 1), jnp.float32)
    for j in range(rows // step):
        hit = hits[:, j * step : (j + 1) * step]
        count = jnp.dot(hit.astype(jnp.bfloat16), upper, preferred_element_type=jnp.float32) + carry
        carry = count[:, step - 1 : step]
        rank[:, j * step : (j + 1) * step] = jnp.where(hit > 0.0, count - 1.0, -1.0).astype(jnp.int32)

    pl.semaphore_wait(barrier, n_dp + 1)

    def pick(to):
        chosen = jnp.where(rank[pl.ds(to, 1), :] == iota((cap, rows), 0), 1.0, 0.0).astype(jnp.bfloat16)
        packed = jnp.dot(chosen, emb_ref[...], preferred_element_type=jnp.float32).astype(jnp.bfloat16)
        keys = lax.dot_general(tags[...], chosen, NT, preferred_element_type=jnp.float32)
        return packed, keys.astype(jnp.bfloat16)

    def x_copy(h, to, slot):
        return pltpu.make_async_remote_copy(
            src_ref=x_out.at[h, to],
            dst_ref=x_in.at[h, pl.ds(pl.multiple_of(slot * cap, cap), cap), :],
            send_sem=x_ss.at[h, to],
            recv_sem=x_rs.at[h, slot],
            device_id=(to, mm),
            device_id_type=MESH,
        )

    def k_copy(to, slot):
        return pltpu.make_async_remote_copy(
            src_ref=k_out.at[to],
            dst_ref=k_in.at[slot],
            send_sem=k_ss.at[to],
            recv_sem=k_rs.at[slot],
            device_id=(to, mm),
            device_id_type=MESH,
        )

    def partner(k):
        half = (k + 1) // 2
        return lax.rem(me + n_dp // 2 + half * (1 - 2 * (k % 2)), n_dp)

    def send(k, none):
        to = partner(k)
        packed, keys = pick(to)
        k_out[to] = keys
        for h in range(PARTS):
            x_out[h, to] = packed[:, h * part : (h + 1) * part]
        k_copy(to, me).start()
        x_copy(0, to, me).start()
        return none

    lax.fori_loop(0, n_dp - 1, send, 0)
    for h in range(1, PARTS):
        def send_later(k, none, h=h):
            x_copy(h, partner(k), me).start()
            return none

        lax.fori_loop(0, n_dp - 1, send_later, 0)
    packed, keys = pick(me)
    k_in[me] = keys
    for h in range(PARTS):
        x_in[h, pl.ds(pl.multiple_of(me * cap, cap), cap), :] = packed[:, h * part : (h + 1) * part]

    def take_keys(k, none):
        k_copy(partner(k), partner(k)).wait_recv()
        return none

    lax.fori_loop(0, n_dp - 1, take_keys, 0)

    span = cols + 2 * REACH
    for s in range(n_dp):
        key = k_in[s].astype(jnp.float32)
        gap = (iota((span, cap), 0) - REACH).astype(jnp.float32) - key[0:1, :]
        cw[:, s * cap : (s + 1) * cap] = weight(gap) * key[2:3, :]
        rm[:, s * cap : (s + 1) * cap] = jnp.where(
            iota((band, cap), 0).astype(jnp.float32) == key[1:2, :], 1.0, 0.0
        ).astype(jnp.bfloat16)

    def fill(a, none):
        line = jnp.broadcast_to(cw[pl.ds(a, 1), :], (band, slots)).astype(jnp.bfloat16)
        mix[pl.ds(pl.multiple_of(a * band, band), band), :] = line * rm[...]
        return none

    lax.fori_loop(0, span, fill, 0)
    den = lax.dot_general(
        cw[...].astype(jnp.bfloat16), rm[...], NT, preferred_element_type=jnp.float32
    )
    d_out[0] = den[:REACH]
    d_out[1] = den[REACH + cols :]
    d_own[...] = den[REACH : REACH + cols]

    def h_copy(h, side):
        return pltpu.make_async_remote_copy(
            src_ref=h_out.at[h, side],
            dst_ref=h_in.at[h, 1 - side],
            send_sem=h_ss.at[h, side],
            recv_sem=h_rs.at[h, 1 - side],
            device_id=((left, right)[side], mm),
            device_id_type=MESH,
        )

    def d_copy(side):
        return pltpu.make_async_remote_copy(
            src_ref=d_out.at[side],
            dst_ref=d_in.at[1 - side],
            send_sem=d_ss.at[side],
            recv_sem=d_rs.at[1 - side],
            device_id=((left, right)[side], mm),
            device_id_type=MESH,
        )

    def m_copy(h, side):
        start = 0 if side == 0 else band - REACH
        return pltpu.make_async_remote_copy(
            src_ref=t1.at[h, :, pl.ds(start, REACH), :],
            dst_ref=m_in.at[h, 1 - side],
            send_sem=m_ss.at[h, side],
            recv_sem=m_rs.at[h, 1 - side],
            device_id=(me, (up, down)[side]),
            device_id_type=MESH,
        )

    def dm_copy(side):
        return pltpu.make_async_remote_copy(
            src_ref=d_own,
            dst_ref=dm_in.at[1 - side],
            send_sem=dm_ss.at[side],
            recv_sem=dm_rs.at[1 - side],
            device_id=(me, (up, down)[side]),
            device_id_type=MESH,
        )

    has_dp = (me > 0, me < n_dp - 1)
    has_map = (mm > 0, mm < n_map - 1)

    for side in range(2):
        @pl.when(has_dp[side])
        def _(side=side):
            d_copy(side).start()

    for h in range(PARTS):
        def take(k, none, h=h):
            x_copy(h, partner(k), partner(k)).wait_recv()
            return none

        lax.fori_loop(0, n_dp - 1, take, 0)
        for side in range(2):
            base = 0 if side == 0 else (REACH + cols) * band
            h_out[h, side] = jnp.dot(
                mix[base : base + edge, :], x_in[h], preferred_element_type=jnp.float32
            ).astype(jnp.bfloat16)

            @pl.when(has_dp[side])
            def _(side=side, h=h):
                h_copy(h, side).start()

        def keep(g, none, h=h):
            at = pl.multiple_of(g * edge, edge)
            own[h, pl.ds(at, edge), :] = jnp.dot(
                mix[pl.ds(pl.multiple_of(edge + at, edge), edge), :],
                x_in[h],
                preferred_element_type=jnp.float32,
            )
            return none

        lax.fori_loop(0, cols // REACH, keep, 0)

    for side in range(2):
        base = 0 if side == 0 else cols - REACH

        @pl.when(has_dp[side])
        def _(side=side, base=base):
            d_copy(1 - side).wait_recv()
            d_own[pl.ds(base, REACH), :] += d_in[side]

    for side in range(2):
        @pl.when(has_map[side])
        def _(side=side):
            dm_copy(side).start()

    for h in range(PARTS):
        for side in range(2):
            base = 0 if side == 0 else (cols - REACH) * band

            @pl.when(has_dp[side])
            def _(side=side, base=base, h=h):
                h_copy(h, 1 - side).wait_recv()
                own[h, pl.ds(base, edge), :] += h_in[h, side].astype(jnp.float32)

        t1[h] = own[h].astype(jnp.bfloat16).reshape(cols, band, part)
        for side in range(2):
            @pl.when(has_map[side])
            def _(side=side, h=h):
                m_copy(h, side).start()

        ext_ref[:, REACH : REACH + band, h * part : (h + 1) * part] = t1[h]
    den_ref[1] = d_own[...]

    for side in range(2):
        base = 0 if side == 0 else REACH + band

        @pl.when(has_map[side])
        def _(side=side, base=base):
            dm_copy(1 - side).wait_recv()
            den_ref[2 * side] = dm_in[side]
            for h in range(PARTS):
                m_copy(h, 1 - side).wait_recv()
                ext_ref[:, base : base + REACH, h * part : (h + 1) * part] = m_in[h, side]

        @pl.when(jnp.logical_not(has_map[side]))
        def _(side=side, base=base):
            den_ref[2 * side] = jnp.zeros((cols, band), jnp.float32)
            ext_ref[:, base : base + REACH, :] = jnp.zeros((cols, REACH, width), jnp.bfloat16)

    def sent(k, none):
        k_copy(partner(k), me).wait_send()
        for h in range(PARTS):
            x_copy(h, partner(k), me).wait_send()
        return none

    lax.fori_loop(0, n_dp - 1, sent, 0)
    for side in range(2):
        @pl.when(has_dp[side])
        def _(side=side):
            d_copy(side).wait_send()
            for h in range(PARTS):
                h_copy(h, side).wait_send()

        @pl.when(has_map[side])
        def _(side=side):
            dm_copy(side).wait_send()
            for h in range(PARTS):
                m_copy(h, side).wait_send()


def finish_kernel(ext_ref, den_ref, book_ref, new_ref, copy_ref):
    count, band, width = book_ref.shape
    reach_band = ext_ref.shape[1]
    gap = iota((band, reach_band), 0) + REACH - iota((band, reach_band), 1)
    smooth = weight(gap.astype(jnp.float32)).astype(jnp.bfloat16)
    den = jnp.zeros((band, count), jnp.float32)
    apart = (iota((band, band), 0) - iota((band, band), 1)).astype(jnp.float32)
    for p in range(3):
        taps = weight(apart + float((1 - p) * band)).astype(jnp.bfloat16).astype(jnp.float32)
        den += lax.dot_general(
            taps, den_ref[p], NT, precision=lax.Precision.HIGHEST, preferred_element_type=jnp.float32
        )
    scale = 0.9 / (den + 1.0)
    for i in range(count):
        num = jnp.dot(smooth, ext_ref[i], preferred_element_type=jnp.float32)
        book = book_ref[i]
        new = 0.1 * book + (num + book) * scale[:, i : i + 1]
        new_ref[i] = new
        copy_ref[i] = new.astype(jnp.bfloat16)


def on_device(embeddings, winners, codebook):
    cols, band, width = codebook.shape
    n_dp = lax.axis_size("dp")
    n_map = lax.axis_size("map")
    rows = embeddings.shape[0]
    cap = max(2, 2 * rows // (n_dp * n_map))
    slots = n_dp * cap
    part = width // PARTS
    span = cols + 2 * REACH
    edge = REACH * band
    bf16, f32 = jnp.bfloat16, jnp.float32
    vmem = pl.BlockSpec(memory_space=pltpu.VMEM)
    dma = pltpu.SemaphoreType.DMA
    ext, den = pl.pallas_call(
        functools.partial(exchange_kernel, (n_dp, n_map, cap, cols, band, rows, width)),
        out_shape=(
            jax.ShapeDtypeStruct((cols, band + 2 * REACH, width), bf16),
            jax.ShapeDtypeStruct((3, cols, band), f32),
        ),
        in_specs=[vmem, vmem],
        out_specs=(vmem, vmem),
        scratch_shapes=[
            pltpu.VMEM((n_dp, rows), jnp.int32),
            pltpu.VMEM((16, rows), bf16),
            pltpu.VMEM((PARTS, n_dp, cap, part), bf16),
            pltpu.VMEM((PARTS, slots, part), bf16),
            pltpu.VMEM((n_dp, 16, cap), bf16),
            pltpu.VMEM((n_dp, 16, cap), bf16),
            pltpu.VMEM((span, slots), f32),
            pltpu.VMEM((band, slots), bf16),
            pltpu.VMEM((span * band, slots), bf16),
            pltpu.VMEM((PARTS, cols * band, part), f32),
            pltpu.VMEM((PARTS, 2, edge, part), bf16),
            pltpu.VMEM((PARTS, 2, edge, part), bf16),
            pltpu.VMEM((2, REACH, band), f32),
            pltpu.VMEM((2, REACH, band), f32),
            pltpu.VMEM((cols, band), f32),
            pltpu.VMEM((PARTS, cols, band, part), bf16),
            pltpu.VMEM((PARTS, 2, cols, REACH, part), bf16),
            pltpu.VMEM((2, cols, band), f32),
            dma((PARTS, n_dp)), dma((PARTS, n_dp)), dma((n_dp,)), dma((n_dp,)),
            dma((PARTS, 2)), dma((PARTS, 2)), dma((2,)), dma((2,)),
            dma((PARTS, 2)), dma((PARTS, 2)), dma((2,)), dma((2,)),
        ],
        compiler_params=pltpu.CompilerParams(
            collective_id=0, has_side_effects=True, vmem_limit_bytes=50 * 1024 * 1024
        ),
        cost_estimate=pl.CostEstimate(
            flops=2 * width * slots * (rows + span * band),
            bytes_accessed=2 * width * (rows + cols * (band + 2 * REACH)),
            transcendentals=span * slots,
        ),
    )(embeddings, winners.reshape(1, rows))

    step = 8 if cols % 8 == 0 else cols
    return pl.pallas_call(
        finish_kernel,
        grid=(cols // step,),
        out_shape=(
            jax.ShapeDtypeStruct((cols, band, width), f32),
            jax.ShapeDtypeStruct((cols, band, width), bf16),
        ),
        in_specs=[
            pl.BlockSpec((step, band + 2 * REACH, width), lambda i: (i, 0, 0)),
            pl.BlockSpec((3, step, band), lambda i: (0, i, 0)),
            pl.BlockSpec((step, band, width), lambda i: (i, 0, 0)),
        ],
        out_specs=(
            pl.BlockSpec((step, band, width), lambda i: (i, 0, 0)),
            pl.BlockSpec((step, band, width), lambda i: (i, 0, 0)),
        ),
        compiler_params=pltpu.CompilerParams(vmem_limit_bytes=32 * 1024 * 1024),
    )(ext, den, codebook)


def solution(mesh):
    placed = (P("dp", None), P("dp"), P("dp", "map", None))
    return jax.shard_map(
        on_device,
        mesh=mesh,
        in_specs=placed,
        out_specs=(P("dp", "map", None), P("dp", "map", None)),
        check_vma=False,
    )
```

time: 170 us -> 63.8 us (0.38)
  the two profiles are of different devices: /device:TPU:1 before, /device:TPU:13 now
where the time goes in v1:
time: 63.8 us; the launch traced here: 63.5 us
  Pallas kernels  60.6 us (95%)
  local copies, waits for them, and re-layouts  2.3 us (4%)
  between operations  0.66 us (1%)
    pallas_call x1, Pallas kernels, on_device(): pl.pallas_call(functools.partial(exchange_kernel, (n_dp, n_map, cap, cols...  57.4 us
    pallas_call x1, Pallas kernels, on_device(): pl.pallas_call(finish_kernel, grid=(cols // step,), out_shape=(jax.ShapeD...  3.12 us
    unnamed x6, local copies, waits for them, and re-layouts  2.3 us

profile of v1, /device:TPU:13, one launch (start us, length us, event | category | flops | bytes accessed | tf_op | source)
XLA Modules:
  0.0 63.5 jit_solution(477881061080972366)
XLA Ops:
  0.6 0.0 copy-start.1
  0.6 1.6 %copy-done.1 = bf16[4096,256]{1,0:T(8,128)(2,1)S(1)} copy-done((bf16[4096,256]{1,0:T(8,128)(2,1)S(1)}, bf16[4096,256]{1,0:T(8,128)(2,1)}, u32[]{:S(2)}) %copy-start.1) | copy-done | bytes 2097176
  2.2 0.0 copy-start.2
  2.2 0.7 %copy-done.2 = s32[4096]{0:T(1024)S(1)} copy-done((s32[4096]{0:T(1024)S(1)}, s32[4096]{0:T(1024)}, u32[]{:S(2)}) %copy-start.2) | copy-done | bytes 16408
  2.9 0.0 copy-start
  2.9 57.4 %shard_map.50 = (bf16[32,96,256]{2,1,0:T(8,128)(2,1)S(1)}, f32[3,32,64]{2,1,0:T(8,128)S(1)}) custom-call(bf16[4096,256]{1,0:T(8,128)(2,1)S(1)} %copy-done.1, s32[1,4096]{1,0:T(1,128)S(1)} %bitcast.1), custom_call_target="tpu_custom_call" | custom-call | flops 8589934592 | bytes 3670016 | tf_op jit(solution)/shard_map/pallas_call | solution.py:337
  60.4 0.0 copy-done
  60.4 3.1 %shard_map.51 = (f32[32,64,256]{2,1,0:T(8,128)}, bf16[32,64,256]{2,1,0:T(8,128)(2,1)}) custom-call(bf16[32,96,256]{2,1,0:T(8,128)(2,1)S(1)} %get-tuple-element.4.ext_ref, f32[3,32,64]{2,1,0:T(8,128)S(1)} %get-tuple-element.5.den_ref, f32[32,64,256]{2,1,0:T(8,128)S(1)} %copy-done), custom_call_target="tpu_custom_call" | custom-call | tf_op jit(solution)/shard_map/pallas_call | solution.py:379
Async XLA Ops:
  0.6 1.6 %copy-start.1 = (bf16[4096,256]{1,0:T(8,128)(2,1)S(1)}, bf16[4096,256]{1,0:T(8,128)(2,1)}, u32[]{:S(2)}) copy-start(bf16[4096,256]{1,0:T(8,128)(2,1)} %emb_ref.1) | copy-start | bytes 6291460
  2.2 0.7 %copy-start.2 = (s32[4096]{0:T(1024)S(1)}, s32[4096]{0:T(1024)}, u32[]{:S(2)}) copy-start(s32[4096]{0:T(1024)} %param.4) | copy-start | bytes 49156
  2.9 57.5 %copy-start = (f32[32,64,256]{2,1,0:T(8,128)S(1)}, f32[32,64,256]{2,1,0:T(8,128)}, u32[]{:S(2)}) copy-start(f32[32,64,256]{2,1,0:T(8,128)} %book_ref.1) | copy-start | bytes 6291460

commit v2 on v1

v2 whole, which is shorter than its diff:
```python
import functools

import jax
import jax.numpy as jnp
from jax import lax
from jax.experimental import pallas as pl
from jax.experimental.pallas import tpu as pltpu
from jax.sharding import PartitionSpec as P

REACH = 16
SIGMA = float(REACH) / 2.0
HALVES = 2
MESH = pl.DeviceIdType.MESH
NT = (((1,), (1,)), ((), ()))


def iota(shape, dim):
    return lax.broadcasted_iota(jnp.int32, shape, dim)


def over(values, size):
    if size & (size - 1) == 0:
        return lax.shift_right_logical(values, jnp.int32(size.bit_length() - 1))
    return values // size


def weight(gap):
    apart = gap / SIGMA
    return jnp.where(jnp.abs(gap) <= REACH, jnp.exp(-0.5 * apart * apart) / SIGMA, 0.0)


def exchange_kernel(
    dims, emb_hbm, win_ref, ext_ref, den_ref,
    emb, rank, tags, x_out, x_in, k_out, k_in, cw, rm, mix, acc, h_out, h_in, d_out, d_in, d_own, y_out, t1, m_in,
    dm_in, e_sem, x_ss, x_rs, k_ss, k_rs, h_ss, h_rs, d_ss, d_rs, y_ss, y_rs, m_ss, m_rs, dm_ss, dm_rs,
):
    n_dp, n_map, cap, cols, band, rows, width = dims
    part = width // HALVES
    edge = REACH * band
    groups = cols // REACH
    pairs = n_dp // 2
    me = lax.axis_index("dp")
    mm = lax.axis_index("map")
    pair, mine = me // 2, me % 2
    mate = 2 * pair + 1 - mine
    left, right = lax.rem(me + n_dp - 2, n_dp), lax.rem(me + 2, n_dp)
    up, down = lax.rem(mm + n_map - 1, n_map), lax.rem(mm + 1, n_map)
    has_dp = (pair > 0, pair < pairs - 1)
    has_map = (mm > 0, mm < n_map - 1)

    fetch = pltpu.make_async_copy(emb_hbm, emb, e_sem)
    fetch.start()
    barrier = pltpu.get_barrier_semaphore()
    for k in range(1, n_dp):
        pl.semaphore_signal(
            barrier, inc=1, device_id=(lax.rem(me + k, n_dp), mm), device_id_type=MESH
        )
    for other in (up, down):
        pl.semaphore_signal(barrier, inc=1, device_id=(me, other), device_id_type=MESH)

    win = win_ref[...]
    column = over(win, band * n_map)
    row_of = win - column * (band * n_map) - mm * band
    target = over(column, cols)
    local = column - target * cols
    inside = (row_of >= 0) & (row_of < band)
    target = jnp.where(inside, target, -1)
    which = iota((16, rows), 0)
    tags[...] = jnp.where(
        which == 0,
        local.astype(jnp.float32),
        jnp.where(which == 1, row_of.astype(jnp.float32), jnp.where(which == 2, 1.0, 0.0)),
    ).astype(jnp.bfloat16)
    step = 256
    upper = jnp.where(iota((step, step), 0) <= iota((step, step), 1), 1.0, 0.0).astype(jnp.bfloat16)
    hits = jnp.where(target == iota((n_dp, rows), 0), 1.0, 0.0)
    carry = jnp.zeros((n_dp, 1), jnp.float32)
    for j in range(rows // step):
        hit = hits[:, j * step : (j + 1) * step]
        count = jnp.dot(hit.astype(jnp.bfloat16), upper, preferred_element_type=jnp.float32) + carry
        carry = count[:, step - 1 : step]
        rank[:, j * step : (j + 1) * step] = jnp.where(hit > 0.0, count - 1.0, -1.0).astype(jnp.int32)

    fetch.wait()
    pl.semaphore_wait(barrier, n_dp + 1)

    def plane(s):
        half = (s + 1) // 2
        return lax.rem(pair + pairs // 2 + half * (1 - 2 * (s % 2)), pairs)

    def place(s, sender):
        return pl.ds(pl.multiple_of((2 * s + sender) * cap, cap), cap)

    def x_copy(s, tile, to, sender):
        return pltpu.make_async_remote_copy(
            src_ref=x_out.at[s, to, tile],
            dst_ref=x_in.at[tile, place(s, sender), :],
            send_sem=x_ss.at[s, to, tile],
            recv_sem=x_rs.at[s, sender, tile],
            device_id=(2 * plane(s) + to, mm),
            device_id_type=MESH,
        )

    def k_copy(s, tile, to, sender):
        return pltpu.make_async_remote_copy(
            src_ref=k_out.at[s, tile],
            dst_ref=k_in.at[s, sender, tile],
            send_sem=k_ss.at[s, to, tile],
            recv_sem=k_rs.at[s, sender, tile],
            device_id=(2 * plane(s) + to, mm),
            device_id_type=MESH,
        )

    def pick(s, tile):
        to = 2 * plane(s) + tile
        chosen = jnp.where(rank[pl.ds(to, 1), :] == iota((cap, rows), 0), 1.0, 0.0).astype(jnp.bfloat16)
        packed = jnp.dot(chosen, emb[...], preferred_element_type=jnp.float32).astype(jnp.bfloat16)
        keys = lax.dot_general(tags[...], chosen, NT, preferred_element_type=jnp.float32)
        k_out[s, tile] = keys.astype(jnp.bfloat16)
        for h in range(HALVES):
            x_out[s, h, tile] = packed[:, h * part : (h + 1) * part]

    last = pairs - 1

    def send(i, none):
        s, tile = i // 2, i % 2
        pick(s, tile)

        @pl.when(s < last)
        def _():
            for to in range(2):
                k_copy(s, tile, to, mine).start()
                x_copy(s, tile, to, mine).start()

        @pl.when(s == last)
        def _():
            k_copy(s, tile, 1 - mine, mine).start()
            x_copy(s, tile, 1 - mine, mine).start()
            k_in[s, mine, tile] = k_out[s, tile]
            x_in[tile, place(s, mine), :] = x_out[s, mine, tile]

        return none

    lax.fori_loop(0, 2 * pairs, send, 0)
    acc[...] = jnp.zeros_like(acc)

    span = cols + 2 * REACH

    def take(s, senders):
        for sender in senders:
            for tile in range(2):
                k_copy(s, tile, 1 - mine, sender).wait_recv()
                x_copy(s, tile, 1 - mine, sender).wait_recv()
        for sender in range(2):
            for tile in range(2):
                key = k_in[s, sender, tile].astype(jnp.float32)
                gap = (iota((span, cap), 0) - REACH).astype(jnp.float32) - key[0:1, :]
                cw[tile, s, :, sender * cap : (sender + 1) * cap] = weight(gap) * key[2:3, :]
                rm[tile, s, :, sender * cap : (sender + 1) * cap] = jnp.where(
                    iota((band, cap), 0).astype(jnp.float32) == key[1:2, :], 1.0, 0.0
                ).astype(jnp.bfloat16)

    def contract(s, tile, g):
        lines = rm[tile, s]
        for i in range(REACH):
            line = jnp.broadcast_to(cw[tile, s, pl.ds(g * REACH + i, 1), :], (band, 2 * cap))
            mix[i * band : (i + 1) * band, :] = line.astype(jnp.bfloat16) * lines
        acc[tile * groups + g] += jnp.dot(
            mix[...],
            x_in[tile, pl.ds(pl.multiple_of(2 * s * cap, 2 * cap), 2 * cap), :],
            preferred_element_type=jnp.float32,
        )

    def add_step(s):
        def one(i, none):
            contract(s, i // (groups + 2), i % (groups + 2))
            return none

        lax.fori_loop(0, 2 * (groups + 2), one, 0)

    take(last, (1 - mine,))
    add_step(last)

    def middle_steps(s, none):
        take(s, (0, 1))
        add_step(s)
        return none

    lax.fori_loop(0, last - 1, middle_steps, 0)
    final = last - 1
    take(final, (0, 1))

    def h_copy(side):
        return pltpu.make_async_remote_copy(
            src_ref=h_out.at[side],
            dst_ref=h_in.at[1 - side],
            send_sem=h_ss.at[side],
            recv_sem=h_rs.at[1 - side],
            device_id=((left, right)[side], mm),
            device_id_type=MESH,
        )

    def d_copy(side):
        return pltpu.make_async_remote_copy(
            src_ref=d_out.at[side],
            dst_ref=d_in.at[1 - side],
            send_sem=d_ss.at[side],
            recv_sem=d_rs.at[1 - side],
            device_id=((left, right)[side], mm),
            device_id_type=MESH,
        )

    def y_copy(slot, cg):
        return pltpu.make_async_remote_copy(
            src_ref=y_out.at[slot],
            dst_ref=t1.at[cg, mine],
            send_sem=y_ss.at[slot],
            recv_sem=y_rs.at[slot],
            device_id=(mate, mm),
            device_id_type=MESH,
        )

    def m_copy(side, cg, h):
        start = 0 if side == 0 else band - REACH
        return pltpu.make_async_remote_copy(
            src_ref=t1.at[cg, h, :, pl.ds(start, REACH), :],
            dst_ref=m_in.at[1 - side, cg, h],
            send_sem=m_ss.at[side, cg, h],
            recv_sem=m_rs.at[1 - side, cg, h],
            device_id=(me, (up, down)[side]),
            device_id_type=MESH,
        )

    def m_start(cg, h):
        for side in range(2):
            @pl.when(has_map[side])
            def _(side=side):
                m_copy(side, cg, h).start()

    def dm_copy(side):
        return pltpu.make_async_remote_copy(
            src_ref=d_own,
            dst_ref=dm_in.at[1 - side],
            send_sem=dm_ss.at[side],
            recv_sem=dm_rs.at[1 - side],
            device_id=(me, (up, down)[side]),
            device_id_type=MESH,
        )

    for side in range(2):
        contract(final, side, 0 if side == 0 else groups + 1)
        h_out[side] = acc[0 if side == 0 else 2 * groups + 1].astype(jnp.bfloat16)

        @pl.when(has_dp[side])
        def _(side=side):
            h_copy(side).start()

    def inner(i, none):
        tile = i // groups
        contract(final, tile, i % groups + 2 * (1 - tile))
        return none

    lax.fori_loop(0, 2 * groups, inner, 0)
    block = (REACH, band, part)
    for m in range(groups - 1):
        y_out[m] = acc[2 + m + (1 - mine) * (groups - 1)].astype(jnp.bfloat16).reshape(block)
        y_copy(m, m + mine).start()
        t1[m + 1 - mine, mine] = acc[2 + m + mine * (groups - 1)].astype(jnp.bfloat16).reshape(block)
        m_start(m + 1 - mine, mine)
    contract(final, 0, 1)
    contract(final, 1, groups)

    totals = []
    for tile in range(2):
        total = jnp.zeros((span, band), jnp.float32)
        for s in range(pairs):
            total += lax.dot_general(
                cw[tile, s].astype(jnp.bfloat16), rm[tile, s], NT, preferred_element_type=jnp.float32
            )
        totals.append(total)
    d_out[0] = totals[0][:REACH]
    d_out[1] = totals[1][REACH + cols :]
    d_own[...] = jnp.where(
        mine == 0, totals[0][REACH : REACH + cols], totals[1][REACH : REACH + cols]
    )
    d_own[pl.ds(pl.multiple_of((1 - mine) * (cols - REACH), 8), REACH), :] += jnp.where(
        mine == 0, totals[1][:REACH], totals[0][REACH + cols :]
    )
    for side in range(2):
        @pl.when(has_dp[side])
        def _(side=side):
            d_copy(side).start()

    for side in range(2):
        @pl.when(has_dp[side])
        def _(side=side):
            h_copy(1 - side).wait_recv()
            acc[1 if side == 0 else 2 * groups] += h_in[side].astype(jnp.float32)

    tip = groups - 1
    y_out[tip] = acc[1 + (1 - mine) * (2 * groups - 1)].astype(jnp.bfloat16).reshape(block)
    y_copy(tip, (1 - mine) * (groups - 1)).start()
    own_tip = mine * (groups - 1)
    t1[own_tip, mine] = acc[1 + mine * (2 * groups - 1)].astype(jnp.bfloat16).reshape(block)
    m_start(own_tip, mine)

    for side in range(2):
        @pl.when(has_dp[side])
        def _(side=side):
            d_copy(1 - side).wait_recv()

        @pl.when(has_dp[side] & (mine == side))
        def _(side=side):
            base = 0 if side == 0 else cols - REACH
            d_own[pl.ds(base, REACH), :] += d_in[side]

    for side in range(2):
        @pl.when(has_map[side])
        def _(side=side):
            dm_copy(side).start()

    for m in range(groups - 1):
        y_copy(m, m + mine).wait_recv()
        m_start(m + 1 - mine, 1 - mine)
    y_copy(tip, own_tip).wait_recv()
    m_start(own_tip, 1 - mine)

    for cg in range(groups):
        for h in range(HALVES):
            ext_ref[cg * REACH : (cg + 1) * REACH, REACH : REACH + band, h * part : (h + 1) * part] = t1[cg, h]
    den_ref[1] = d_own[...]

    for side in range(2):
        base = 0 if side == 0 else REACH + band

        @pl.when(has_map[side])
        def _(side=side, base=base):
            dm_copy(1 - side).wait_recv()
            den_ref[2 * side] = dm_in[side]
            for cg in range(groups):
                for h in range(HALVES):
                    m_copy(1 - side, cg, h).wait_recv()
                    ext_ref[
                        cg * REACH : (cg + 1) * REACH, base : base + REACH, h * part : (h + 1) * part
                    ] = m_in[side, cg, h]

        @pl.when(jnp.logical_not(has_map[side]))
        def _(side=side, base=base):
            den_ref[2 * side] = jnp.zeros((cols, band), jnp.float32)
            ext_ref[:, base : base + REACH, :] = jnp.zeros((cols, REACH, width), jnp.bfloat16)

    def sent(i, none):
        s, tile = i // 2, i % 2
        for to in range(2):
            @pl.when((s < last) | (mine != to))
            def _(to=to):
                k_copy(s, tile, to, mine).wait_send()
                x_copy(s, tile, to, mine).wait_send()

        return none

    lax.fori_loop(0, 2 * pairs, sent, 0)
    for cg in range(groups):
        y_copy(cg, 0).wait_send()
    for side in range(2):
        @pl.when(has_dp[side])
        def _(side=side):
            d_copy(side).wait_send()
            h_copy(side).wait_send()

        @pl.when(has_map[side])
        def _(side=side):
            dm_copy(side).wait_send()
            for cg in range(groups):
                for h in range(HALVES):
                    m_copy(side, cg, h).wait_send()


def finish_kernel(ext_ref, den_ref, book_ref, new_ref, copy_ref):
    count, band, width = book_ref.shape
    reach_band = ext_ref.shape[1]
    gap = iota((band, reach_band), 0) + REACH - iota((band, reach_band), 1)
    smooth = weight(gap.astype(jnp.float32)).astype(jnp.bfloat16)
    den = jnp.zeros((band, count), jnp.float32)
    apart = (iota((band, band), 0) - iota((band, band), 1)).astype(jnp.float32)
    for p in range(3):
        taps = weight(apart + float((1 - p) * band)).astype(jnp.bfloat16).astype(jnp.float32)
        den += lax.dot_general(
            taps, den_ref[p], NT, precision=lax.Precision.HIGHEST, preferred_element_type=jnp.float32
        )
    scale = 0.9 / (den + 1.0)
    for i in range(count):
        num = jnp.dot(smooth, ext_ref[i], preferred_element_type=jnp.float32)
        book = book_ref[i]
        new = 0.1 * book + (num + book) * scale[:, i : i + 1]
        new_ref[i] = new
        copy_ref[i] = new.astype(jnp.bfloat16)


def on_device(embeddings, winners, codebook):
    cols, band, width = codebook.shape
    n_dp = lax.axis_size("dp")
    n_map = lax.axis_size("map")
    rows = embeddings.shape[0]
    cap = max(2, 2 * rows // (n_dp * n_map))
    slots = n_dp * cap
    part = width // HALVES
    pairs = n_dp // 2
    groups = cols // REACH
    span = cols + 2 * REACH
    edge = REACH * band
    bf16, f32 = jnp.bfloat16, jnp.float32
    vmem = pl.BlockSpec(memory_space=pltpu.VMEM)
    dma = pltpu.SemaphoreType.DMA
    ext, den = pl.pallas_call(
        functools.partial(exchange_kernel, (n_dp, n_map, cap, cols, band, rows, width)),
        out_shape=(
            jax.ShapeDtypeStruct((cols, band + 2 * REACH, width), bf16),
            jax.ShapeDtypeStruct((3, cols, band), f32),
        ),
        in_specs=[pl.BlockSpec(memory_space=pl.ANY), vmem],
        out_specs=(vmem, vmem),
        scratch_shapes=[
            pltpu.VMEM((rows, width), bf16),
            pltpu.VMEM((n_dp, rows), jnp.int32),
            pltpu.VMEM((16, rows), bf16),
            pltpu.VMEM((pairs, HALVES, 2, cap, part), bf16),
            pltpu.VMEM((2, slots, part), bf16),
            pltpu.VMEM((pairs, 2, 16, cap), bf16),
            pltpu.VMEM((pairs, 2, 2, 16, cap), bf16),
            pltpu.VMEM((2, pairs, span, 2 * cap), f32),
            pltpu.VMEM((2, pairs, band, 2 * cap), bf16),
            pltpu.VMEM((edge, 2 * cap), bf16),
            pltpu.VMEM((2 * groups + 2, edge, part), f32),
            pltpu.VMEM((2, edge, part), bf16),
            pltpu.VMEM((2, edge, part), bf16),
            pltpu.VMEM((2, REACH, band), f32),
            pltpu.VMEM((2, REACH, band), f32),
            pltpu.VMEM((cols, band), f32),
            pltpu.VMEM((groups, REACH, band, part), bf16),
            pltpu.VMEM((groups, HALVES, REACH, band, part), bf16),
            pltpu.VMEM((2, groups, HALVES, REACH, REACH, part), bf16),
            pltpu.VMEM((2, cols, band), f32),
            dma,
            dma((pairs, 2, 2)), dma((pairs, 2, 2)), dma((pairs, 2, 2)), dma((pairs, 2, 2)),
            dma((2,)), dma((2,)), dma((2,)), dma((2,)), dma((groups,)), dma((groups,)),
            dma((2, groups, HALVES)), dma((2, groups, HALVES)), dma((2,)), dma((2,)),
        ],
        compiler_params=pltpu.CompilerParams(
            collective_id=0, has_side_effects=True, vmem_limit_bytes=50 * 1024 * 1024
        ),
        cost_estimate=pl.CostEstimate(
            flops=2 * width * slots * (rows + span * band),
            bytes_accessed=2 * width * (rows + cols * (band + 2 * REACH)),
            transcendentals=span * slots,
        ),
    )(embeddings, winners.reshape(1, rows))

    step = 8 if cols % 8 == 0 else cols
    return pl.pallas_call(
        finish_kernel,
        grid=(cols // step,),
        out_shape=(
            jax.ShapeDtypeStruct((cols, band, width), f32),
            jax.ShapeDtypeStruct((cols, band, width), bf16),
        ),
        in_specs=[
            pl.BlockSpec((step, band + 2 * REACH, width), lambda i: (i, 0, 0)),
            pl.BlockSpec((3, step, band), lambda i: (0, i, 0)),
            pl.BlockSpec((step, band, width), lambda i: (i, 0, 0)),
        ],
        out_specs=(
            pl.BlockSpec((step, band, width), lambda i: (i, 0, 0)),
            pl.BlockSpec((step, band, width), lambda i: (i, 0, 0)),
        ),
        compiler_params=pltpu.CompilerParams(vmem_limit_bytes=32 * 1024 * 1024),
    )(ext, den, codebook)


def solution(mesh):
    placed = (P("dp", None), P("dp"), P("dp", "map", None))
    return jax.shard_map(
        on_device,
        mesh=mesh,
        in_specs=placed,
        out_specs=(P("dp", "map", None), P("dp", "map", None)),
        check_vma=False,
    )
```

time: 63.8 us -> 61.5 us (0.964)
  the two profiles are of different devices: /device:TPU:13 before, /device:TPU:1 now
where the time goes in v2:
time: 61.5 us; the launch traced here: 61.3 us
  Pallas kernels  58.3 us (95%)
  local copies, waits for them, and re-layouts  2.3 us (4%)
  between operations  0.66 us (1%)
    pallas_call x1, Pallas kernels, on_device(): pl.pallas_call(functools.partial(exchange_kernel, (n_dp, n_map, cap, cols...  55.2 us
    pallas_call x1, Pallas kernels, on_device(): pl.pallas_call(finish_kernel, grid=(cols // step,), out_shape=(jax.ShapeD...  3.13 us
    unnamed x6, local copies, waits for them, and re-layouts  2.3 us

profile of v2, /device:TPU:1, one launch (start us, length us, event | category | flops | bytes accessed | tf_op | source)
XLA Modules:
  0.0 61.3 jit_solution(12652625757705191860)
XLA Ops:
  0.6 0.0 copy-start.1
  0.6 1.6 %copy-done.1 = bf16[4096,256]{1,0:T(8,128)(2,1)S(1)} copy-done((bf16[4096,256]{1,0:T(8,128)(2,1)S(1)}, bf16[4096,256]{1,0:T(8,128)(2,1)}, u32[]{:S(2)}) %copy-start.1) | copy-done | bytes 2097176
  2.2 0.0 copy-start.2
  2.2 0.7 %copy-done.2 = s32[4096]{0:T(1024)S(1)} copy-done((s32[4096]{0:T(1024)S(1)}, s32[4096]{0:T(1024)}, u32[]{:S(2)}) %copy-start.2) | copy-done | bytes 16408
  2.9 0.0 copy-start
  2.9 55.2 %shard_map.50 = (bf16[32,96,256]{2,1,0:T(8,128)(2,1)S(1)}, f32[3,32,64]{2,1,0:T(8,128)S(1)}) custom-call(bf16[4096,256]{1,0:T(8,128)(2,1)S(1)} %copy-done.1, s32[1,4096]{1,0:T(1,128)S(1)} %bitcast.1), custom_call_target="tpu_custom_call" | custom-call | flops 8589934592 | bytes 3670016 | tf_op jit(solution)/shard_map/pallas_call | solution.py:415
  58.2 0.0 copy-done
  58.2 3.1 %shard_map.51 = (f32[32,64,256]{2,1,0:T(8,128)}, bf16[32,64,256]{2,1,0:T(8,128)(2,1)}) custom-call(bf16[32,96,256]{2,1,0:T(8,128)(2,1)S(1)} %get-tuple-element.4.ext_ref, f32[3,32,64]{2,1,0:T(8,128)S(1)} %get-tuple-element.5.den_ref, f32[32,64,256]{2,1,0:T(8,128)S(1)} %copy-done), custom_call_target="tpu_custom_call" | custom-call | tf_op jit(solution)/shard_map/pallas_call | solution.py:460
Async XLA Ops:
  0.6 1.6 %copy-start.1 = (bf16[4096,256]{1,0:T(8,128)(2,1)S(1)}, bf16[4096,256]{1,0:T(8,128)(2,1)}, u32[]{:S(2)}) copy-start(bf16[4096,256]{1,0:T(8,128)(2,1)} %emb_hbm.1) | copy-start | bytes 6291460
  2.2 0.7 %copy-start.2 = (s32[4096]{0:T(1024)S(1)}, s32[4096]{0:T(1024)}, u32[]{:S(2)}) copy-start(s32[4096]{0:T(1024)} %param.4) | copy-start | bytes 49156
  2.9 55.2 %copy-start = (f32[32,64,256]{2,1,0:T(8,128)S(1)}, f32[32,64,256]{2,1,0:T(8,128)}, u32[]{:S(2)}) copy-start(f32[32,64,256]{2,1,0:T(8,128)} %book_ref.1) | copy-start | bytes 6291460

commit v3 on v2

--- a/solution.py
+++ b/solution.py
@@ -31,12 +31,11 @@
 
 def exchange_kernel(
     dims, emb_hbm, win_ref, ext_ref, den_ref,
-    emb, rank, tags, x_out, x_in, k_out, k_in, cw, rm, mix, acc, h_out, h_in, d_out, d_in, d_own, y_out, t1, m_in,
+    emb, rank, tags, x_out, x_in, k_out, k_in, oc, rm, mix, acc, raw, h_in, mid, tips, d_ext, d_own, y_out, t1, m_in,
     dm_in, e_sem, x_ss, x_rs, k_ss, k_rs, h_ss, h_rs, d_ss, d_rs, y_ss, y_rs, m_ss, m_rs, dm_ss, dm_rs,
 ):
     n_dp, n_map, cap, cols, band, rows, width = dims
     part = width // HALVES
-    edge = REACH * band
     groups = cols // REACH
     pairs = n_dp // 2
     me = lax.axis_index("dp")
@@ -65,12 +64,7 @@
     local = column - target * cols
     inside = (row_of >= 0) & (row_of < band)
     target = jnp.where(inside, target, -1)
-    which = iota((16, rows), 0)
-    tags[...] = jnp.where(
-        which == 0,
-        local.astype(jnp.float32),
-        jnp.where(which == 1, row_of.astype(jnp.float32), jnp.where(which == 2, 1.0, 0.0)),
-    ).astype(jnp.bfloat16)
+    tags[...] = (local * band + row_of + 1).astype(jnp.float32)
     step = 256
     upper = jnp.where(iota((step, step), 0) <= iota((step, step), 1), 1.0, 0.0).astype(jnp.bfloat16)
     hits = jnp.where(target == iota((n_dp, rows), 0), 1.0, 0.0)
@@ -113,10 +107,12 @@
 
     def pick(s, tile):
         to = 2 * plane(s) + tile
-        chosen = jnp.where(rank[pl.ds(to, 1), :] == iota((cap, rows), 0), 1.0, 0.0).astype(jnp.bfloat16)
+        match = rank[pl.ds(to, 1), :] == iota((cap, rows), 0)
+        chosen = jnp.where(match, 1.0, 0.0).astype(jnp.bfloat16)
         packed = jnp.dot(chosen, emb[...], preferred_element_type=jnp.float32).astype(jnp.bfloat16)
-        keys = lax.dot_general(tags[...], chosen, NT, preferred_element_type=jnp.float32)
-        k_out[s, tile] = keys.astype(jnp.bfloat16)
+        key = jnp.sum(jnp.where(match, tags[...], 0.0), axis=1, keepdims=True)
+        turned = jnp.where(iota((cap, cap), 0) == iota((cap, cap), 1), key, 0.0)
+        k_out[s, tile] = jnp.broadcast_to(jnp.sum(turned, axis=0, keepdims=True), (8, cap))
         for h in range(HALVES):
             x_out[s, h, tile] = packed[:, h * part : (h + 1) * part]
 
@@ -144,7 +140,8 @@
     lax.fori_loop(0, 2 * pairs, send, 0)
     acc[...] = jnp.zeros_like(acc)
 
-    span = cols + 2 * REACH
+    lot = min(band, 1024 // cols)
+    lots = band // lot
 
     def take(s, senders):
         for sender in senders:
@@ -153,19 +150,18 @@
                 x_copy(s, tile, 1 - mine, sender).wait_recv()
         for sender in range(2):
             for tile in range(2):
-                key = k_in[s, sender, tile].astype(jnp.float32)
-                gap = (iota((span, cap), 0) - REACH).astype(jnp.float32) - key[0:1, :]
-                cw[tile, s, :, sender * cap : (sender + 1) * cap] = weight(gap) * key[2:3, :]
-                rm[tile, s, :, sender * cap : (sender + 1) * cap] = jnp.where(
-                    iota((band, cap), 0).astype(jnp.float32) == key[1:2, :], 1.0, 0.0
-                ).astype(jnp.bfloat16)
-
-    def contract(s, tile, g):
-        lines = rm[tile, s]
-        for i in range(REACH):
-            line = jnp.broadcast_to(cw[tile, s, pl.ds(g * REACH + i, 1), :], (band, 2 * cap))
-            mix[i * band : (i + 1) * band, :] = line.astype(jnp.bfloat16) * lines
-        acc[tile * groups + g] += jnp.dot(
+                key = k_in[s, sender, tile][0:1, :].astype(jnp.int32) - 1
+                at = over(key, band)
+                lanes = slice(sender * cap, (sender + 1) * cap)
+                oc[tile, s, :, lanes] = jnp.where(iota((cols, cap), 0) == at, 1.0, 0.0).astype(jnp.bfloat16)
+                rm[tile, s, :, lanes] = jnp.where(iota((band, cap), 0) == key - at * band, 1.0, 0.0)
+
+    def contract(s, tile, j):
+        lines = oc[tile, s]
+        for i in range(lot):
+            line = jnp.broadcast_to(rm[tile, s, pl.ds(j * lot + i, 1), :], (cols, 2 * cap))
+            mix[i * cols : (i + 1) * cols, :] = line.astype(jnp.bfloat16) * lines
+        acc[tile, pl.ds(pl.multiple_of(j * lot * cols, lot * cols), lot * cols), :] += jnp.dot(
             mix[...],
             x_in[tile, pl.ds(pl.multiple_of(2 * s * cap, 2 * cap), 2 * cap), :],
             preferred_element_type=jnp.float32,
@@ -173,10 +169,10 @@
 
     def add_step(s):
         def one(i, none):
-            contract(s, i // (groups + 2), i % (groups + 2))
+            contract(s, i // lots, i % lots)
             return none
 
-        lax.fori_loop(0, 2 * (groups + 2), one, 0)
+        lax.fori_loop(0, 2 * lots, one, 0)
 
     take(last, (1 - mine,))
     add_step(last)
@@ -186,13 +182,11 @@
         add_step(s)
         return none
 
-    lax.fori_loop(0, last - 1, middle_steps, 0)
-    final = last - 1
-    take(final, (0, 1))
+    lax.fori_loop(0, last, middle_steps, 0)
 
     def h_copy(side):
         return pltpu.make_async_remote_copy(
-            src_ref=h_out.at[side],
+            src_ref=raw.at[side, :, pl.ds(0 if side == 0 else cols - REACH, REACH), :],
             dst_ref=h_in.at[1 - side],
             send_sem=h_ss.at[side],
             recv_sem=h_rs.at[1 - side],
@@ -202,8 +196,8 @@
 
     def d_copy(side):
         return pltpu.make_async_remote_copy(
-            src_ref=d_out.at[side],
-            dst_ref=d_in.at[1 - side],
+            src_ref=d_ext.at[pl.ds(REACH if side == 0 else 2 * cols, REACH), :],
+            dst_ref=d_ext.at[pl.ds(REACH + 2 * cols if side == 0 else 0, REACH), :],
             send_sem=d_ss.at[side],
             recv_sem=d_rs.at[1 - side],
             device_id=((left, right)[side], mm),
@@ -248,72 +242,103 @@
         )
 
     for side in range(2):
-        contract(final, side, 0 if side == 0 else groups + 1)
-        h_out[side] = acc[0 if side == 0 else 2 * groups + 1].astype(jnp.bfloat16)
+        raw[side] = acc[side].astype(jnp.bfloat16).reshape(band, cols, part)
 
         @pl.when(has_dp[side])
         def _(side=side):
             h_copy(side).start()
 
-    def inner(i, none):
-        tile = i // groups
-        contract(final, tile, i % groups + 2 * (1 - tile))
-        return none
-
-    lax.fori_loop(0, 2 * groups, inner, 0)
-    block = (REACH, band, part)
-    for m in range(groups - 1):
-        y_out[m] = acc[2 + m + (1 - mine) * (groups - 1)].astype(jnp.bfloat16).reshape(block)
-        y_copy(m, m + mine).start()
-        t1[m + 1 - mine, mine] = acc[2 + m + mine * (groups - 1)].astype(jnp.bfloat16).reshape(block)
-        m_start(m + 1 - mine, mine)
-    contract(final, 0, 1)
-    contract(final, 1, groups)
-
-    totals = []
+        @pl.when(jnp.logical_not(has_dp[side]))
+        def _(side=side):
+            h_in[side] = jnp.zeros((band, REACH, part), jnp.bfloat16)
+            d_ext[pl.ds(0 if side == 0 else REACH + 2 * cols, REACH), :] = jnp.zeros((REACH, band), jnp.float32)
+
     for tile in range(2):
-        total = jnp.zeros((span, band), jnp.float32)
+        total = jnp.zeros((cols, band), jnp.float32)
         for s in range(pairs):
             total += lax.dot_general(
-                cw[tile, s].astype(jnp.bfloat16), rm[tile, s], NT, preferred_element_type=jnp.float32
+                oc[tile, s], rm[tile, s].astype(jnp.bfloat16), NT, preferred_element_type=jnp.float32
             )
-        totals.append(total)
-    d_out[0] = totals[0][:REACH]
-    d_out[1] = totals[1][REACH + cols :]
-    d_own[...] = jnp.where(
-        mine == 0, totals[0][REACH : REACH + cols], totals[1][REACH : REACH + cols]
+        d_ext[REACH + tile * cols : REACH + (tile + 1) * cols, :] = total
+    for side in range(2):
+        @pl.when(has_dp[side])
+        def _(side=side):
+            d_copy(side).start()
+
+    def smooth(taps, parts_of, out):
+        size = taps.shape[0]
+
+        def rows_at(i, none):
+            ext = jnp.concatenate(
+                [jnp.concatenate(parts_of(4 * i + j), axis=0) for j in range(4)], axis=1
+            )
+            got = jnp.dot(taps, ext, preferred_element_type=jnp.float32)
+            for j in range(4):
+                out[pl.ds(pl.multiple_of((4 * i + j) * size, size), size), :] = got[
+                    :, j * part : (j + 1) * part
+                ]
+            return none
+
+        lax.fori_loop(0, band // 4, rows_at, 0)
+
+    def share(low, high):
+        first = mine == 0
+        return (
+            jnp.where(first, low, high).astype(jnp.bfloat16),
+            jnp.where(first, high, low).astype(jnp.bfloat16),
+        )
+
+    inner = groups - 1
+    if inner:
+        size = 2 * inner * REACH
+        gap = iota((size, 2 * cols), 0) + REACH - iota((size, 2 * cols), 1)
+        taps = weight(gap.astype(jnp.float32)).astype(jnp.bfloat16)
+        smooth(taps, lambda r: [raw[0, r], raw[1, r]], mid)
+        for m in range(inner):
+            for i in range(REACH):
+                kept, given = share(
+                    mid[pl.ds(m * REACH + i, band, stride=size), :],
+                    mid[pl.ds((m + inner) * REACH + i, band, stride=size), :],
+                )
+                t1[m + 1 - mine, mine, i] = kept
+                y_out[m, i] = given
+            y_copy(m, m + mine).start()
+            m_start(m + 1 - mine, mine)
+
+    size = 2 * REACH
+    reached = 2 * cols + 2 * REACH
+    place_of = iota((size, reached), 0)
+    place_of = jnp.where(place_of < REACH, place_of, place_of + 2 * cols - 2 * REACH)
+    taps = weight((place_of + REACH - iota((size, reached), 1)).astype(jnp.float32)).astype(jnp.bfloat16)
+    for side in range(2):
+        @pl.when(has_dp[side])
+        def _(side=side):
+            h_copy(1 - side).wait_recv()
+
+    smooth(taps, lambda r: [h_in[0, r], raw[0, r], raw[1, r], h_in[1, r]], tips)
+    tip = groups - 1
+    own_tip = mine * (groups - 1)
+    for i in range(REACH):
+        kept, given = share(
+            tips[pl.ds(i, band, stride=size), :], tips[pl.ds(REACH + i, band, stride=size), :]
+        )
+        t1[own_tip, mine, i] = kept
+        y_out[tip, i] = given
+    y_copy(tip, (1 - mine) * (groups - 1)).start()
+    m_start(own_tip, mine)
+
+    for side in range(2):
+        @pl.when(has_dp[side])
+        def _(side=side):
+            d_copy(1 - side).wait_recv()
+
+    gap = iota((cols, reached), 0) + mine * cols + REACH - iota((cols, reached), 1)
+    d_own[...] = jnp.dot(
+        weight(gap.astype(jnp.float32)).astype(jnp.bfloat16).astype(jnp.float32),
+        d_ext[...],
+        precision=lax.Precision.HIGHEST,
+        preferred_element_type=jnp.float32,
     )
-    d_own[pl.ds(pl.multiple_of((1 - mine) * (cols - REACH), 8), REACH), :] += jnp.where(
-        mine == 0, totals[1][:REACH], totals[0][REACH + cols :]
-    )
-    for side in range(2):
-        @pl.when(has_dp[side])
-        def _(side=side):
-            d_copy(side).start()
-
-    for side in range(2):
-        @pl.when(has_dp[side])
-        def _(side=side):
-            h_copy(1 - side).wait_recv()
-            acc[1 if side == 0 else 2 * groups] += h_in[side].astype(jnp.float32)
-
-    tip = groups - 1
-    y_out[tip] = acc[1 + (1 - mine) * (2 * groups - 1)].astype(jnp.bfloat16).reshape(block)
-    y_copy(tip, (1 - mine) * (groups - 1)).start()
-    own_tip = mine * (groups - 1)
-    t1[own_tip, mine] = acc[1 + mine * (2 * groups - 1)].astype(jnp.bfloat16).reshape(block)
-    m_start(own_tip, mine)
-
-    for side in range(2):
-        @pl.when(has_dp[side])
-        def _(side=side):
-            d_copy(1 - side).wait_recv()
-
-        @pl.when(has_dp[side] & (mine == side))
-        def _(side=side):
-            base = 0 if side == 0 else cols - REACH
-            d_own[pl.ds(base, REACH), :] += d_in[side]
-
     for side in range(2):
         @pl.when(has_map[side])
         def _(side=side):
@@ -407,8 +432,6 @@
     part = width // HALVES
     pairs = n_dp // 2
     groups = cols // REACH
-    span = cols + 2 * REACH
-    edge = REACH * band
     bf16, f32 = jnp.bfloat16, jnp.float32
     vmem = pl.BlockSpec(memory_space=pltpu.VMEM)
     dma = pltpu.SemaphoreType.DMA
@@ -423,19 +446,20 @@
         scratch_shapes=[
             pltpu.VMEM((rows, width), bf16),
             pltpu.VMEM((n_dp, rows), jnp.int32),
-            pltpu.VMEM((16, rows), bf16),
+            pltpu.VMEM((1, rows), f32),
             pltpu.VMEM((pairs, HALVES, 2, cap, part), bf16),
             pltpu.VMEM((2, slots, part), bf16),
-            pltpu.VMEM((pairs, 2, 16, cap), bf16),
-            pltpu.VMEM((pairs, 2, 2, 16, cap), bf16),
-            pltpu.VMEM((2, pairs, span, 2 * cap), f32),
-            pltpu.VMEM((2, pairs, band, 2 * cap), bf16),
-            pltpu.VMEM((edge, 2 * cap), bf16),
-            pltpu.VMEM((2 * groups + 2, edge, part), f32),
-            pltpu.VMEM((2, edge, part), bf16),
-            pltpu.VMEM((2, edge, part), bf16),
-            pltpu.VMEM((2, REACH, band), f32),
-            pltpu.VMEM((2, REACH, band), f32),
+            pltpu.VMEM((pairs, 2, 8, cap), f32),
+            pltpu.VMEM((pairs, 2, 2, 8, cap), f32),
+            pltpu.VMEM((2, pairs, cols, 2 * cap), bf16),
+            pltpu.VMEM((2, pairs, band, 2 * cap), f32),
+            pltpu.VMEM((min(band, 1024 // cols) * cols, 2 * cap), bf16),
+            pltpu.VMEM((2, band * cols, part), f32),
+            pltpu.VMEM((2, band, cols, part), bf16),
+            pltpu.VMEM((2, band, REACH, part), bf16),
+            pltpu.VMEM((band * max(1, 2 * (groups - 1)) * REACH, part), f32),
+            pltpu.VMEM((band * 2 * REACH, part), f32),
+            pltpu.VMEM((2 * cols + 2 * REACH, band), f32),
             pltpu.VMEM((cols, band), f32),
             pltpu.VMEM((groups, REACH, band, part), bf16),
             pltpu.VMEM((groups, HALVES, REACH, band, part), bf16),
@@ -447,12 +471,12 @@
             dma((2, groups, HALVES)), dma((2, groups, HALVES)), dma((2,)), dma((2,)),
         ],
         compiler_params=pltpu.CompilerParams(
-            collective_id=0, has_side_effects=True, vmem_limit_bytes=50 * 1024 * 1024
+            collective_id=0, has_side_effects=True, vmem_limit_bytes=60 * 1024 * 1024
         ),
         cost_estimate=pl.CostEstimate(
-            flops=2 * width * slots * (rows + span * band),
+            flops=2 * width * slots * (rows + cols * band),
             bytes_accessed=2 * width * (rows + cols * (band + 2 * REACH)),
-            transcendentals=span * slots,
+            transcendentals=0,
         ),
     )(embeddings, winners.reshape(1, rows))
 
@@ -473,7 +497,7 @@
             pl.BlockSpec((step, band, width), lambda i: (i, 0, 0)),
             pl.BlockSpec((step, band, width), lambda i: (i, 0, 0)),
         ),
-        compiler_params=pltpu.CompilerParams(vmem_limit_bytes=32 * 1024 * 1024),
+        compiler_params=pltpu.CompilerParams(vmem_limit_bytes=60 * 1024 * 1024),
     )(ext, den, codebook)
 
 

time: 61.5 us -> 63.7 us (1.036)
  Pallas kernels: 58.3 us -> 62.8 us
  local copies, waits for them, and re-layouts: 2.3 us -> 0 us
    pallas_call x1, Pallas kernels: 55.2 us -> 57.7 us  [on_device(): pl.pallas_call(functools.partial(exchange_kernel, (n_dp, n_map, cap, cols...]
    unnamed x6 -> x0, local copies, waits for them, and re-layouts: 2.3 us -> none
    pallas_call x1, Pallas kernels: 3.13 us -> 5.16 us  [on_device(): pl.pallas_call(finish_kernel, grid=(cols // step,), out_shape=(jax.ShapeD...]
where the time goes in v3:
time: 63.7 us; the launch traced here: 63.5 us
  Pallas kernels  62.8 us (99%)
  between operations  0.64 us (1%)
    pallas_call x1, Pallas kernels, on_device(): pl.pallas_call(functools.partial(exchange_kernel, (n_dp, n_map, cap, cols...  57.7 us
    pallas_call x1, Pallas kernels, on_device(): pl.pallas_call(finish_kernel, grid=(cols // step,), out_shape=(jax.ShapeD...  5.16 us

profile of v3, /device:TPU:1, one launch (start us, length us, event | category | flops | bytes accessed | tf_op | source)
XLA Modules:
  0.0 63.5 jit_solution(5065334722951025476)
XLA Ops:
  0.6 57.7 %shard_map.50 = (bf16[32,96,256]{2,1,0:T(8,128)(2,1)}, f32[3,32,64]{2,1,0:T(8,128)}) custom-call(bf16[4096,256]{1,0:T(8,128)(2,1)} %emb_hbm.1, s32[1,4096]{1,0:T(1,128)} %bitcast.1), custom_call_target="tpu_custom_call" | custom-call | flops 6442450944 | bytes 3670016 | tf_op jit(solution)/shard_map/pallas_call | solution.py:438
  58.3 5.2 %shard_map.51 = (f32[32,64,256]{2,1,0:T(8,128)}, bf16[32,64,256]{2,1,0:T(8,128)(2,1)}) custom-call(bf16[32,96,256]{2,1,0:T(8,128)(2,1)} %get-tuple-element.4.ext_ref, f32[3,32,64]{2,1,0:T(8,128)} %get-tuple-element.5.den_ref, f32[32,64,256]{2,1,0:T(8,128)} %book_ref.1), custom_call_target="tpu_custom_call" | custom-call | tf_op jit(solution)/shard_map/pallas_call | solution.py:484

commit v4 on v2

v4 whole, which is shorter than its diff:
```python
import functools

import jax
import jax.numpy as jnp
from jax import lax
from jax.experimental import pallas as pl
from jax.experimental.pallas import tpu as pltpu
from jax.sharding import PartitionSpec as P

REACH = 16
SIGMA = float(REACH) / 2.0
HALVES = 2
UNIT = REACH // 2
MESH = pl.DeviceIdType.MESH
NT = (((1,), (1,)), ((), ()))


def iota(shape, dim):
    return lax.broadcasted_iota(jnp.int32, shape, dim)


def over(values, size):
    if size & (size - 1) == 0:
        return lax.shift_right_logical(values, jnp.int32(size.bit_length() - 1))
    return values // size


def weight(gap):
    apart = gap / SIGMA
    return jnp.where(jnp.abs(gap) <= REACH, jnp.exp(-0.5 * apart * apart) / SIGMA, 0.0)


def exchange_kernel(
    dims, emb_hbm, win_ref, num_ref, scale_ref,
    emb, rank, tags, x_out, x_in, k_out, k_in, cw, rm, mix, acc, h_out, h_in, d_out, d_in, d_own, y_out, t1, m_in,
    dm_in, e_sem, x_ss, x_rs, k_ss, k_rs, h_ss, h_rs, d_ss, d_rs, y_ss, y_rs, m_ss, m_rs, dm_ss, dm_rs,
):
    n_dp, n_map, cap, cols, band, rows, width = dims
    part = width // HALVES
    unit = UNIT * band
    over_units = REACH // UNIT
    col_units = cols // UNIT
    spare = col_units - over_units
    span_units = col_units + 2 * over_units
    pairs = n_dp // 2
    me = lax.axis_index("dp")
    mm = lax.axis_index("map")
    pair, mine = me // 2, me % 2
    mate = 2 * pair + 1 - mine
    left, right = lax.rem(me + n_dp - 2, n_dp), lax.rem(me + 2, n_dp)
    up, down = lax.rem(mm + n_map - 1, n_map), lax.rem(mm + 1, n_map)
    has_dp = (pair > 0, pair < pairs - 1)
    has_map = (mm > 0, mm < n_map - 1)

    fetch = pltpu.make_async_copy(emb_hbm, emb, e_sem)
    fetch.start()
    barrier = pltpu.get_barrier_semaphore()
    for k in range(1, n_dp):
        pl.semaphore_signal(
            barrier, inc=1, device_id=(lax.rem(me + k, n_dp), mm), device_id_type=MESH
        )
    for other in (up, down):
        pl.semaphore_signal(barrier, inc=1, device_id=(me, other), device_id_type=MESH)

    win = win_ref[...]
    column = over(win, band * n_map)
    row_of = win - column * (band * n_map) - mm * band
    target = over(column, cols)
    local = column - target * cols
    inside = (row_of >= 0) & (row_of < band)
    target = jnp.where(inside, target, -1)
    tags[...] = (local * band + row_of + 1).astype(jnp.float32)
    step = 256
    upper = jnp.where(iota((step, step), 0) <= iota((step, step), 1), 1.0, 0.0).astype(jnp.bfloat16)
    hits = jnp.where(target == iota((n_dp, rows), 0), 1.0, 0.0)
    carry = jnp.zeros((n_dp, 1), jnp.float32)
    for j in range(rows // step):
        hit = hits[:, j * step : (j + 1) * step]
        count = jnp.dot(hit.astype(jnp.bfloat16), upper, preferred_element_type=jnp.float32) + carry
        carry = count[:, step - 1 : step]
        rank[:, j * step : (j + 1) * step] = jnp.where(hit > 0.0, count - 1.0, -1.0).astype(jnp.int32)

    fetch.wait()
    pl.semaphore_wait(barrier, n_dp + 1)

    def plane(s):
        half = (s + 1) // 2
        return lax.rem(pair + pairs // 2 + half * (1 - 2 * (s % 2)), pairs)

    def place(s, sender):
        return pl.ds(pl.multiple_of((2 * s + sender) * cap, cap), cap)

    def x_copy(s, tile, to, sender):
        return pltpu.make_async_remote_copy(
            src_ref=x_out.at[s, to, tile],
            dst_ref=x_in.at[tile, place(s, sender), :],
            send_sem=x_ss.at[s, to, tile],
            recv_sem=x_rs.at[s, sender, tile],
            device_id=(2 * plane(s) + to, mm),
            device_id_type=MESH,
        )

    def k_copy(s, tile, to, sender):
        return pltpu.make_async_remote_copy(
            src_ref=k_out.at[s, tile],
            dst_ref=k_in.at[s, sender, tile],
            send_sem=k_ss.at[s, to, tile],
            recv_sem=k_rs.at[s, sender, tile],
            device_id=(2 * plane(s) + to, mm),
            device_id_type=MESH,
        )

    def pick(s, tile):
        to = 2 * plane(s) + tile
        match = rank[pl.ds(to, 1), :] == iota((cap, rows), 0)
        chosen = jnp.where(match, 1.0, 0.0).astype(jnp.bfloat16)
        packed = jnp.dot(chosen, emb[...], preferred_element_type=jnp.float32).astype(jnp.bfloat16)
        key = jnp.sum(jnp.where(match, tags[...], 0.0), axis=1, keepdims=True)
        turned = jnp.where(iota((cap, cap), 0) == iota((cap, cap), 1), key, 0.0)
        k_out[s, tile] = jnp.broadcast_to(jnp.sum(turned, axis=0, keepdims=True), (8, cap))
        for h in range(HALVES):
            x_out[s, h, tile] = packed[:, h * part : (h + 1) * part]

    last = pairs - 1

    def send(i, none):
        s, tile = i // 2, i % 2
        pick(s, tile)

        @pl.when(s < last)
        def _():
            for to in range(2):
                k_copy(s, tile, to, mine).start()
                x_copy(s, tile, to, mine).start()

        @pl.when(s == last)
        def _():
            k_copy(s, tile, 1 - mine, mine).start()
            x_copy(s, tile, 1 - mine, mine).start()
            k_in[s, mine, tile] = k_out[s, tile]
            x_in[tile, place(s, mine), :] = x_out[s, mine, tile]

        return none

    lax.fori_loop(0, 2 * pairs, send, 0)
    acc[...] = jnp.zeros_like(acc)

    span = cols + 2 * REACH

    def take(s, senders):
        for sender in senders:
            for tile in range(2):
                k_copy(s, tile, 1 - mine, sender).wait_recv()
                x_copy(s, tile, 1 - mine, sender).wait_recv()
        for sender in range(2):
            for tile in range(2):
                key = k_in[s, sender, tile][0:1, :].astype(jnp.int32) - 1
                at = over(key, band)
                gap = (iota((span, cap), 0) - REACH - at).astype(jnp.float32)
                lanes = slice(sender * cap, (sender + 1) * cap)
                cw[tile, s, :, lanes] = weight(gap)
                rm[tile, s, :, lanes] = jnp.where(
                    iota((band, cap), 0) == key - at * band, 1.0, 0.0
                ).astype(jnp.bfloat16)

    def contract(s, tile, g, count):
        lines = rm[tile, s]
        for i in range(UNIT * count):
            line = jnp.broadcast_to(cw[tile, s, pl.ds(g * UNIT + i, 1), :], (band, 2 * cap))
            mix[i * band : (i + 1) * band, :] = line.astype(jnp.bfloat16) * lines
        at = pl.multiple_of((tile * col_units + g) * unit, unit)
        acc[pl.ds(at, unit * count), :] += jnp.dot(
            mix[pl.ds(0, unit * count), :],
            x_in[tile, pl.ds(pl.multiple_of(2 * s * cap, 2 * cap), 2 * cap), :],
            preferred_element_type=jnp.float32,
        )

    def add_step(s):
        count = span_units // over_units

        def one(i, none):
            contract(s, i // count, i % count * over_units, over_units)
            return none

        lax.fori_loop(0, 2 * count, one, 0)

    take(last, (1 - mine,))
    add_step(last)

    def middle_steps(s, none):
        take(s, (0, 1))
        add_step(s)
        return none

    lax.fori_loop(0, last - 1, middle_steps, 0)
    final = last - 1
    take(final, (0, 1))

    def h_copy(side, u):
        return pltpu.make_async_remote_copy(
            src_ref=h_out.at[side, u],
            dst_ref=h_in.at[1 - side, u],
            send_sem=h_ss.at[side, u],
            recv_sem=h_rs.at[1 - side, u],
            device_id=((left, right)[side], mm),
            device_id_type=MESH,
        )

    def d_copy(side):
        return pltpu.make_async_remote_copy(
            src_ref=d_out.at[side],
            dst_ref=d_in.at[1 - side],
            send_sem=d_ss.at[side],
            recv_sem=d_rs.at[1 - side],
            device_id=((left, right)[side], mm),
            device_id_type=MESH,
        )

    def y_copy(slot, to):
        return pltpu.make_async_remote_copy(
            src_ref=y_out.at[slot],
            dst_ref=t1.at[to, mine],
            send_sem=y_ss.at[slot],
            recv_sem=y_rs.at[slot],
            device_id=(mate, mm),
            device_id_type=MESH,
        )

    def m_copy(side, cg, h):
        start = 0 if side == 0 else band - REACH
        return pltpu.make_async_remote_copy(
            src_ref=t1.at[cg, h, :, pl.ds(start, REACH), :],
            dst_ref=m_in.at[1 - side, cg, h],
            send_sem=m_ss.at[side, cg, h],
            recv_sem=m_rs.at[1 - side, cg, h],
            device_id=(me, (up, down)[side]),
            device_id_type=MESH,
        )

    def m_start(cg, h):
        for side in range(2):
            @pl.when(has_map[side])
            def _(side=side):
                m_copy(side, cg, h).start()

    def dm_copy(side):
        return pltpu.make_async_remote_copy(
            src_ref=d_own,
            dst_ref=dm_in.at[1 - side],
            send_sem=dm_ss.at[side],
            recv_sem=dm_rs.at[1 - side],
            device_id=(me, (up, down)[side]),
            device_id_type=MESH,
        )

    for side in range(2):
        @pl.when(jnp.logical_not(has_map[side]))
        def _(side=side):
            dm_in[side] = jnp.zeros((cols, band), jnp.float32)
            m_in[side] = jnp.zeros(m_in.shape[1:], jnp.bfloat16)

    block = (UNIT, band, part)

    def rounded(u):
        at = pl.multiple_of(u * unit, unit)
        return acc[pl.ds(at, unit), :].astype(jnp.bfloat16).reshape(block)

    for u in range(over_units):
        for side in range(2):
            g = u if side == 0 else col_units + over_units + u
            contract(final, side, g, 1)
            h_out[side, u] = rounded(side * col_units + g)

            @pl.when(has_dp[side])
            def _(side=side, u=u):
                h_copy(side, u).start()

    for m in range(spare):
        n = col_units + m - mine * spare
        contract(final, 0, n + over_units, 1)
        contract(final, 1, n - spare, 1)
        y_out[m] = rounded(n + over_units)
        y_copy(m, m + mine * over_units).start()

    for m in range(spare):
        n = over_units + m + mine * spare
        contract(final, 0, n + over_units, 1)
        contract(final, 1, n - spare, 1)
        t1[m + (1 - mine) * over_units, mine] = rounded(n + over_units)
        m_start(m + (1 - mine) * over_units, mine)

    ends = 2 * col_units - over_units
    for e in range(over_units):
        contract(final, 0, e + over_units, 1)
        contract(final, 1, ends + e - spare, 1)
        if e >= spare:
            contract(final, 1, e - spare, 1)
            contract(final, 0, ends + e + over_units, 1)

    totals = []
    for tile in range(2):
        total = jnp.zeros((span, band), jnp.float32)
        for s in range(pairs):
            total += lax.dot_general(
                cw[tile, s].astype(jnp.bfloat16), rm[tile, s], NT, preferred_element_type=jnp.float32
            )
        totals.append(total)
    d_out[0] = totals[0][:REACH]
    d_out[1] = totals[1][REACH + cols :]
    d_own[...] = jnp.where(
        mine == 0, totals[0][REACH : REACH + cols], totals[1][REACH : REACH + cols]
    )
    d_own[pl.ds(pl.multiple_of((1 - mine) * (cols - REACH), 8), REACH), :] += jnp.where(
        mine == 0, totals[1][:REACH], totals[0][REACH + cols :]
    )
    for side in range(2):
        @pl.when(has_dp[side])
        def _(side=side):
            d_copy(side).start()

    for e in range(over_units):
        for side in range(2):
            @pl.when(has_dp[side])
            def _(side=side, e=e):
                h_copy(1 - side, e).wait_recv()
                at = (over_units + e if side == 0 else over_units + ends + e) * unit
                acc[pl.ds(at, unit), :] += h_in[side, e].reshape(unit, part).astype(jnp.float32)

        y_out[spare + e] = rounded(over_units + e + (1 - mine) * ends)
        y_copy(spare + e, e + (1 - mine) * spare).start()
        t1[e + mine * spare, mine] = rounded(over_units + e + mine * ends)
        m_start(e + mine * spare, mine)

    for side in range(2):
        @pl.when(has_dp[side])
        def _(side=side):
            d_copy(1 - side).wait_recv()

        @pl.when(has_dp[side] & (mine == side))
        def _(side=side):
            base = 0 if side == 0 else cols - REACH
            d_own[pl.ds(base, REACH), :] += d_in[side]

    for side in range(2):
        @pl.when(has_map[side])
        def _(side=side):
            dm_copy(side).start()

    gap = iota((band, band + 2 * REACH), 0) + REACH - iota((band, band + 2 * REACH), 1)
    taps = weight(gap.astype(jnp.float32)).astype(jnp.bfloat16)

    def finish(u, h):
        for side in range(2):
            @pl.when(has_map[side])
            def _(side=side):
                m_copy(1 - side, u, h).wait_recv()

        for i in range(0, UNIT, 2):
            ext = jnp.concatenate(
                [
                    jnp.concatenate([m_in[0, u, h, i + k], t1[u, h, i + k], m_in[1, u, h, i + k]], axis=0)
                    for k in range(2)
                ],
                axis=1,
            )
            got = jnp.dot(taps, ext, preferred_element_type=jnp.float32).astype(jnp.bfloat16)
            for k in range(2):
                num_ref[u * UNIT + i + k, :, pl.ds(pl.multiple_of(h * part, part), part)] = got[
                    :, k * part : (k + 1) * part
                ]

    for m in range(spare):
        y_copy(m, 0).wait_recv()
        m_start(m + (1 - mine) * over_units, 1 - mine)
    for m in range(spare):
        finish(m + (1 - mine) * over_units, mine)
    for side in range(2):
        @pl.when(has_map[side])
        def _(side=side):
            dm_copy(1 - side).wait_recv()

    den = jnp.zeros((cols, band), jnp.float32)
    apart = (iota((band, band), 0) - iota((band, band), 1)).astype(jnp.float32)
    for p, counts in enumerate((dm_in[0], d_own[...], dm_in[1])):
        row_taps = weight(apart + float((1 - p) * band)).astype(jnp.bfloat16).astype(jnp.float32)
        den += lax.dot_general(
            counts, row_taps, NT, precision=lax.Precision.HIGHEST, preferred_element_type=jnp.float32
        )
    scale_ref[...] = 0.9 / (den + 1.0)
    for e in range(over_units):
        finish(e + mine * spare, mine)
    for m in range(spare):
        finish(m + (1 - mine) * over_units, 1 - mine)
    for e in range(over_units):
        y_copy(spare + e, 0).wait_recv()
        m_start(e + mine * spare, 1 - mine)
    for e in range(over_units):
        finish(e + mine * spare, 1 - mine)

    def sent(i, none):
        s, tile = i // 2, i % 2
        for to in range(2):
            @pl.when((s < last) | (mine != to))
            def _(to=to):
                k_copy(s, tile, to, mine).wait_send()
                x_copy(s, tile, to, mine).wait_send()

        return none

    lax.fori_loop(0, 2 * pairs, sent, 0)
    for u in range(col_units):
        y_copy(u, 0).wait_send()
    for side in range(2):
        @pl.when(has_dp[side])
        def _(side=side):
            d_copy(side).wait_send()
            for u in range(over_units):
                h_copy(side, u).wait_send()

        @pl.when(has_map[side])
        def _(side=side):
            dm_copy(side).wait_send()
            for u in range(col_units):
                for h in range(HALVES):
                    m_copy(side, u, h).wait_send()


def on_device(embeddings, winners, codebook):
    cols, band, width = codebook.shape
    n_dp = lax.axis_size("dp")
    n_map = lax.axis_size("map")
    rows = embeddings.shape[0]
    cap = max(2, 2 * rows // (n_dp * n_map))
    slots = n_dp * cap
    part = width // HALVES
    pairs = n_dp // 2
    units = cols // UNIT
    past = REACH // UNIT
    unit = UNIT * band
    span = cols + 2 * REACH
    bf16, f32 = jnp.bfloat16, jnp.float32
    vmem = pl.BlockSpec(memory_space=pltpu.VMEM)
    dma = pltpu.SemaphoreType.DMA
    num, scale = pl.pallas_call(
        functools.partial(exchange_kernel, (n_dp, n_map, cap, cols, band, rows, width)),
        out_shape=(
            jax.ShapeDtypeStruct((cols, band, width), bf16),
            jax.ShapeDtypeStruct((cols, band), f32),
        ),
        in_specs=[pl.BlockSpec(memory_space=pl.ANY), vmem],
        out_specs=(vmem, vmem),
        scratch_shapes=[
            pltpu.VMEM((rows, width), bf16),
            pltpu.VMEM((n_dp, rows), jnp.int32),
            pltpu.VMEM((1, rows), f32),
            pltpu.VMEM((pairs, HALVES, 2, cap, part), bf16),
            pltpu.VMEM((2, slots, part), bf16),
            pltpu.VMEM((pairs, 2, 8, cap), f32),
            pltpu.VMEM((pairs, 2, 2, 8, cap), f32),
            pltpu.VMEM((2, pairs, span, 2 * cap), f32),
            pltpu.VMEM((2, pairs, band, 2 * cap), bf16),
            pltpu.VMEM((REACH * band, 2 * cap), bf16),
            pltpu.VMEM((2 * (units + past) * unit, part), f32),
            pltpu.VMEM((2, past, UNIT, band, part), bf16),
            pltpu.VMEM((2, past, UNIT, band, part), bf16),
            pltpu.VMEM((2, REACH, band), f32),
            pltpu.VMEM((2, REACH, band), f32),
            pltpu.VMEM((cols, band), f32),
            pltpu.VMEM((units, UNIT, band, part), bf16),
            pltpu.VMEM((units, HALVES, UNIT, band, part), bf16),
            pltpu.VMEM((2, units, HALVES, UNIT, REACH, part), bf16),
            pltpu.VMEM((2, cols, band), f32),
            dma,
            dma((pairs, 2, 2)), dma((pairs, 2, 2)), dma((pairs, 2, 2)), dma((pairs, 2, 2)),
            dma((2, past)), dma((2, past)), dma((2,)), dma((2,)), dma((units,)), dma((units,)),
            dma((2, units, HALVES)), dma((2, units, HALVES)), dma((2,)), dma((2,)),
        ],
        compiler_params=pltpu.CompilerParams(
            collective_id=0, has_side_effects=True, vmem_limit_bytes=56 * 1024 * 1024
        ),
        cost_estimate=pl.CostEstimate(
            flops=2 * width * slots * (rows + span * band),
            bytes_accessed=2 * width * (rows + cols * (band + 2 * REACH)),
            transcendentals=span * slots,
        ),
    )(embeddings, winners.reshape(1, rows))

    updated = 0.1 * codebook + (num.astype(f32) + codebook) * scale[:, :, None]
    return updated, updated.astype(bf16)


def solution(mesh):
    placed = (P("dp", None), P("dp"), P("dp", "map", None))
    return jax.shard_map(
        on_device,
        mesh=mesh,
        in_specs=placed,
        out_specs=(P("dp", "map", None), P("dp", "map", None)),
        check_vma=False,
    )
```

time: 61.5 us -> 60.2 us (0.979)
  other arithmetic: 0 us -> 3.44 us
  Pallas kernels: 58.3 us -> 55.8 us
  local copies, waits for them, and re-layouts: 2.3 us -> 0.01 us
    convert_element_type x0 -> x1, other arithmetic: none -> 3.44 us  [on_device(): return (updated, updated.astype(bf16))]
    pallas_call x1 -> x0, Pallas kernels: 3.13 us -> none  [on_device(): pl.pallas_call(finish_kernel, grid=(cols // step,), out_shape=(jax.ShapeD...]
    unnamed x6 -> x2, local copies, waits for them, and re-layouts: 2.3 us -> 0.01 us
where the time goes in v4:
time: 60.2 us; the launch traced here: 59.9 us
  Pallas kernels  55.8 us (93%)
  other arithmetic  3.44 us (6%)
  between operations  0.65 us (1%)
    pallas_call x1, Pallas kernels, on_device(): pl.pallas_call(functools.partial(exchange_kernel, (n_dp, n_map, cap, cols...  55.8 us
    convert_element_type x1, other arithmetic, on_device(): return (updated, updated.astype(bf16))  3.44 us

profile of v4, /device:TPU:1, one launch (start us, length us, event | category | flops | bytes accessed | tf_op | source)
XLA Modules:
  0.0 59.9 jit_solution(14939604284236547650)
XLA Ops:
  0.6 0.0 copy-start
  0.6 55.8 %shard_map.50 = (bf16[32,64,256]{2,1,0:T(8,128)(2,1)}, f32[32,64]{1,0:T(8,128)}) custom-call(bf16[4096,256]{1,0:T(8,128)(2,1)} %emb_hbm.1, s32[1,4096]{1,0:T(1,128)} %bitcast.1), custom_call_target="tpu_custom_call" | custom-call | flops 8589934592 | bytes 3670016 | tf_op jit(solution)/shard_map/pallas_call | solution.py:444
  56.4 0.0 copy-done
  56.4 3.4 %fusion = (bf16[32,64,256]{2,1,0:T(8,128)(2,1)}, f32[32,64,256]{2,1,0:T(8,128)}) fusion(f32[32,64]{1,0:T(8,128)} %get-tuple-element.5, f32[32,64,256]{2,1,0:T(8,128)S(1)} %copy-done, bf16[32,64,256]{2,1,0:T(8,128)(2,1)} %get-tuple-element.4), kind=kLoop, calls=%fused_computation.1 | loop fusion | flops 3145728 | bytes 6299648 | tf_op jit(solution)/shard_map/convert_element_type | solution.py:489
Async XLA Ops:
  0.6 55.8 %copy-start = (f32[32,64,256]{2,1,0:T(8,128)S(1)}, f32[32,64,256]{2,1,0:T(8,128)}, u32[]{:S(2)}) copy-start(f32[32,64,256]{2,1,0:T(8,128)} %param.5) | copy-start | bytes 6291460

commit v5 on v4

--- a/solution.py
+++ b/solution.py
@@ -32,7 +32,7 @@
 
 def exchange_kernel(
     dims, emb_hbm, win_ref, num_ref, scale_ref,
-    emb, rank, tags, x_out, x_in, k_out, k_in, cw, rm, mix, acc, h_out, h_in, d_out, d_in, d_own, y_out, t1, m_in,
+    emb, rank, keys, x_out, x_in, k_out, k_in, cw, rm, mix, acc, h_out, h_in, d_out, d_in, d_own, y_out, t1, m_in,
     dm_in, e_sem, x_ss, x_rs, k_ss, k_rs, h_ss, h_rs, d_ss, d_rs, y_ss, y_rs, m_ss, m_rs, dm_ss, dm_rs,
 ):
     n_dp, n_map, cap, cols, band, rows, width = dims
@@ -69,7 +69,6 @@
     local = column - target * cols
     inside = (row_of >= 0) & (row_of < band)
     target = jnp.where(inside, target, -1)
-    tags[...] = (local * band + row_of + 1).astype(jnp.float32)
     step = 256
     upper = jnp.where(iota((step, step), 0) <= iota((step, step), 1), 1.0, 0.0).astype(jnp.bfloat16)
     hits = jnp.where(target == iota((n_dp, rows), 0), 1.0, 0.0)
@@ -78,7 +77,27 @@
         hit = hits[:, j * step : (j + 1) * step]
         count = jnp.dot(hit.astype(jnp.bfloat16), upper, preferred_element_type=jnp.float32) + carry
         carry = count[:, step - 1 : step]
-        rank[:, j * step : (j + 1) * step] = jnp.where(hit > 0.0, count - 1.0, -1.0).astype(jnp.int32)
+        rank[:, j * step : (j + 1) * step] = jnp.where(hit > 0.0, count - 1.0, -1.0)
+
+    high = cap // 16
+    slot = jnp.max(rank[...], axis=0, keepdims=True).astype(jnp.int32)
+    where_high = jnp.where(slot >= 0, target * high + over(slot, 16), -1)
+    tall = jnp.where(iota((n_dp * high, rows), 0) == where_high, 1.0, 0.0).astype(jnp.bfloat16)
+    low = iota((16, rows), 0) == slot % 16
+    tags = jnp.concatenate(
+        [jnp.where(low, of.astype(jnp.float32), 0.0) for of in (local, row_of, jnp.ones_like(local))], axis=0
+    ).astype(jnp.bfloat16)
+    table = lax.dot_general(tall, tags, NT, preferred_element_type=jnp.float32)
+    lane = iota((48, cap), 0)
+    spread = jnp.where(
+        lane % 16 == iota((48, cap), 1) % 16, jnp.where(lane < 16, float(band), 1.0), 0.0
+    ).astype(jnp.bfloat16)
+    table = jnp.dot(table.astype(jnp.bfloat16), spread, preferred_element_type=jnp.float32)
+    table = jnp.where(iota((n_dp * high, cap), 0) % high == over(iota((n_dp * high, cap), 1), 16), table, 0.0)
+    join = jnp.where(iota((n_dp, n_dp * high), 0) == over(iota((n_dp, n_dp * high), 1), high), 1.0, 0.0)
+    keys[...] = jnp.dot(
+        join, table, precision=lax.Precision.HIGHEST, preferred_element_type=jnp.float32
+    )
 
     fetch.wait()
     pl.semaphore_wait(barrier, n_dp + 1)
@@ -110,39 +129,67 @@
             device_id_type=MESH,
         )
 
-    def pick(s, tile):
-        to = 2 * plane(s) + tile
-        match = rank[pl.ds(to, 1), :] == iota((cap, rows), 0)
-        chosen = jnp.where(match, 1.0, 0.0).astype(jnp.bfloat16)
-        packed = jnp.dot(chosen, emb[...], preferred_element_type=jnp.float32).astype(jnp.bfloat16)
-        key = jnp.sum(jnp.where(match, tags[...], 0.0), axis=1, keepdims=True)
-        turned = jnp.where(iota((cap, cap), 0) == iota((cap, cap), 1), key, 0.0)
-        k_out[s, tile] = jnp.broadcast_to(jnp.sum(turned, axis=0, keepdims=True), (8, cap))
-        for h in range(HALVES):
-            x_out[s, h, tile] = packed[:, h * part : (h + 1) * part]
-
     last = pairs - 1
 
-    def send(i, none):
+    def send_keys(i, none):
         s, tile = i // 2, i % 2
-        pick(s, tile)
+        k_out[s, tile] = jnp.broadcast_to(keys[pl.ds(2 * plane(s) + tile, 1), :], (8, cap))
 
         @pl.when(s < last)
         def _():
             for to in range(2):
                 k_copy(s, tile, to, mine).start()
-                x_copy(s, tile, to, mine).start()
 
         @pl.when(s == last)
         def _():
             k_copy(s, tile, 1 - mine, mine).start()
-            x_copy(s, tile, 1 - mine, mine).start()
             k_in[s, mine, tile] = k_out[s, tile]
-            x_in[tile, place(s, mine), :] = x_out[s, mine, tile]
 
         return none
 
-    lax.fori_loop(0, 2 * pairs, send, 0)
+    lax.fori_loop(0, 2 * pairs, send_keys, 0)
+    piece = rows // 4
+    slot_of = iota((cap, piece), 0).astype(jnp.float32).astype(jnp.bfloat16)
+    one, nought = jnp.bfloat16(1.0), jnp.bfloat16(0.0)
+
+    def send(s, none):
+        packed = jnp.zeros((2 * cap, width), jnp.float32)
+        for q in range(4):
+            chosen = jnp.concatenate(
+                [
+                    jnp.where(
+                        rank[pl.ds(2 * plane(s) + tile, 1), q * piece : (q + 1) * piece].astype(jnp.bfloat16)
+                        == slot_of,
+                        one,
+                        nought,
+                    )
+                    for tile in range(2)
+                ],
+                axis=0,
+            )
+            packed += jnp.dot(
+                chosen, emb[q * piece : (q + 1) * piece, :], preferred_element_type=jnp.float32
+            )
+        packed = packed.astype(jnp.bfloat16)
+        for tile in range(2):
+            for h in range(HALVES):
+                x_out[s, h, tile] = packed[tile * cap : (tile + 1) * cap, h * part : (h + 1) * part]
+
+        @pl.when(s < last)
+        def _():
+            for tile in range(2):
+                for to in range(2):
+                    x_copy(s, tile, to, mine).start()
+
+        @pl.when(s == last)
+        def _():
+            for tile in range(2):
+                x_copy(s, tile, 1 - mine, mine).start()
+                x_in[tile, place(s, mine), :] = x_out[s, mine, tile]
+
+        return none
+
+    lax.fori_loop(0, pairs, send, 0)
     acc[...] = jnp.zeros_like(acc)
 
     span = cols + 2 * REACH
@@ -451,8 +498,8 @@
         out_specs=(vmem, vmem),
         scratch_shapes=[
             pltpu.VMEM((rows, width), bf16),
-            pltpu.VMEM((n_dp, rows), jnp.int32),
-            pltpu.VMEM((1, rows), f32),
+            pltpu.VMEM((n_dp, rows), f32),
+            pltpu.VMEM((n_dp, cap), f32),
             pltpu.VMEM((pairs, HALVES, 2, cap, part), bf16),
             pltpu.VMEM((2, slots, part), bf16),
             pltpu.VMEM((pairs, 2, 8, cap), f32),

time: 60.2 us -> 59.9 us (level)
  no operation moved by 1% of the time
where the time goes in v5:
time: 59.9 us; the launch traced here: 59.3 us
  Pallas kernels  55.2 us (92%)
  other arithmetic  3.44 us (6%)
  between operations  0.65 us (1%)
    pallas_call x1, Pallas kernels, on_device(): pl.pallas_call(functools.partial(exchange_kernel, (n_dp, n_map, cap, cols...  55.2 us
    convert_element_type x1, other arithmetic, on_device(): return (updated, updated.astype(bf16))  3.44 us

profile of v5, /device:TPU:1, one launch (start us, length us, event | category | flops | bytes accessed | tf_op | source)
XLA Modules:
  0.0 59.3 jit_solution(4385179035099312940)
XLA Ops:
  0.6 0.0 copy-start
  0.6 55.2 %shard_map.50 = (bf16[32,64,256]{2,1,0:T(8,128)(2,1)}, f32[32,64]{1,0:T(8,128)}) custom-call(bf16[4096,256]{1,0:T(8,128)(2,1)} %emb_hbm.1, s32[1,4096]{1,0:T(1,128)} %bitcast.1), custom_call_target="tpu_custom_call" | custom-call | flops 8589934592 | bytes 3670016 | tf_op jit(solution)/shard_map/pallas_call | solution.py:491
  55.9 0.0 copy-done
  55.9 3.4 %fusion = (bf16[32,64,256]{2,1,0:T(8,128)(2,1)}, f32[32,64,256]{2,1,0:T(8,128)}) fusion(f32[32,64]{1,0:T(8,128)} %get-tuple-element.5, f32[32,64,256]{2,1,0:T(8,128)S(1)} %copy-done, bf16[32,64,256]{2,1,0:T(8,128)(2,1)} %get-tuple-element.4), kind=kLoop, calls=%fused_computation.1 | loop fusion | flops 3145728 | bytes 6299648 | tf_op jit(solution)/shard_map/convert_element_type | solution.py:536
Async XLA Ops:
  0.6 55.2 %copy-start = (f32[32,64,256]{2,1,0:T(8,128)S(1)}, f32[32,64,256]{2,1,0:T(8,128)}, u32[]{:S(2)}) copy-start(f32[32,64,256]{2,1,0:T(8,128)} %param.5) | copy-start | bytes 6291460

commit v6 on v5

--- a/solution.py
+++ b/solution.py
@@ -79,26 +79,6 @@
         carry = count[:, step - 1 : step]
         rank[:, j * step : (j + 1) * step] = jnp.where(hit > 0.0, count - 1.0, -1.0)
 
-    high = cap // 16
-    slot = jnp.max(rank[...], axis=0, keepdims=True).astype(jnp.int32)
-    where_high = jnp.where(slot >= 0, target * high + over(slot, 16), -1)
-    tall = jnp.where(iota((n_dp * high, rows), 0) == where_high, 1.0, 0.0).astype(jnp.bfloat16)
-    low = iota((16, rows), 0) == slot % 16
-    tags = jnp.concatenate(
-        [jnp.where(low, of.astype(jnp.float32), 0.0) for of in (local, row_of, jnp.ones_like(local))], axis=0
-    ).astype(jnp.bfloat16)
-    table = lax.dot_general(tall, tags, NT, preferred_element_type=jnp.float32)
-    lane = iota((48, cap), 0)
-    spread = jnp.where(
-        lane % 16 == iota((48, cap), 1) % 16, jnp.where(lane < 16, float(band), 1.0), 0.0
-    ).astype(jnp.bfloat16)
-    table = jnp.dot(table.astype(jnp.bfloat16), spread, preferred_element_type=jnp.float32)
-    table = jnp.where(iota((n_dp * high, cap), 0) % high == over(iota((n_dp * high, cap), 1), 16), table, 0.0)
-    join = jnp.where(iota((n_dp, n_dp * high), 0) == over(iota((n_dp, n_dp * high), 1), high), 1.0, 0.0)
-    keys[...] = jnp.dot(
-        join, table, precision=lax.Precision.HIGHEST, preferred_element_type=jnp.float32
-    )
-
     fetch.wait()
     pl.semaphore_wait(barrier, n_dp + 1)
 
@@ -131,23 +111,6 @@
 
     last = pairs - 1
 
-    def send_keys(i, none):
-        s, tile = i // 2, i % 2
-        k_out[s, tile] = jnp.broadcast_to(keys[pl.ds(2 * plane(s) + tile, 1), :], (8, cap))
-
-        @pl.when(s < last)
-        def _():
-            for to in range(2):
-                k_copy(s, tile, to, mine).start()
-
-        @pl.when(s == last)
-        def _():
-            k_copy(s, tile, 1 - mine, mine).start()
-            k_in[s, mine, tile] = k_out[s, tile]
-
-        return none
-
-    lax.fori_loop(0, 2 * pairs, send_keys, 0)
     piece = rows // 4
     slot_of = iota((cap, piece), 0).astype(jnp.float32).astype(jnp.bfloat16)
     one, nought = jnp.bfloat16(1.0), jnp.bfloat16(0.0)
@@ -189,18 +152,57 @@
 
         return none
 
-    lax.fori_loop(0, pairs, send, 0)
+    lax.fori_loop(0, 1, send, 0)
+
+    high = cap // 16
+    slot = jnp.max(rank[...], axis=0, keepdims=True).astype(jnp.int32)
+    where_high = jnp.where(slot >= 0, target * high + over(slot, 16), -1)
+    tall = jnp.where(iota((n_dp * high, rows), 0) == where_high, 1.0, 0.0).astype(jnp.bfloat16)
+    low = iota((16, rows), 0) == slot % 16
+    tags = jnp.concatenate(
+        [jnp.where(low, of.astype(jnp.float32), 0.0) for of in (local, row_of, jnp.ones_like(local))], axis=0
+    ).astype(jnp.bfloat16)
+    table = lax.dot_general(tall, tags, NT, preferred_element_type=jnp.float32)
+    lane = iota((48, cap), 0)
+    spread = jnp.where(
+        lane % 16 == iota((48, cap), 1) % 16, jnp.where(lane < 16, float(band), 1.0), 0.0
+    ).astype(jnp.bfloat16)
+    table = jnp.dot(table.astype(jnp.bfloat16), spread, preferred_element_type=jnp.float32)
+    table = jnp.where(iota((n_dp * high, cap), 0) % high == over(iota((n_dp * high, cap), 1), 16), table, 0.0)
+    join = jnp.where(iota((n_dp, n_dp * high), 0) == over(iota((n_dp, n_dp * high), 1), high), 1.0, 0.0)
+    keys[...] = jnp.dot(
+        join, table, precision=lax.Precision.HIGHEST, preferred_element_type=jnp.float32
+    )
+
+    def send_keys(i, none):
+        s, tile = i // 2, i % 2
+        k_out[s, tile] = jnp.broadcast_to(keys[pl.ds(2 * plane(s) + tile, 1), :], (8, cap))
+
+        @pl.when(s < last)
+        def _():
+            for to in range(2):
+                k_copy(s, tile, to, mine).start()
+
+        @pl.when(s == last)
+        def _():
+            k_copy(s, tile, 1 - mine, mine).start()
+            k_in[s, mine, tile] = k_out[s, tile]
+
+        return none
+
+    lax.fori_loop(0, 2 * pairs, send_keys, 0)
+    lax.fori_loop(1, pairs, send, 0)
     acc[...] = jnp.zeros_like(acc)
 
     span = cols + 2 * REACH
 
-    def take(s, senders):
+    def take(s, senders, tiles=(0, 1)):
         for sender in senders:
-            for tile in range(2):
+            for tile in tiles:
                 k_copy(s, tile, 1 - mine, sender).wait_recv()
                 x_copy(s, tile, 1 - mine, sender).wait_recv()
         for sender in range(2):
-            for tile in range(2):
+            for tile in tiles:
                 key = k_in[s, sender, tile][0:1, :].astype(jnp.int32) - 1
                 at = over(key, band)
                 gap = (iota((span, cap), 0) - REACH - at).astype(jnp.float32)
@@ -212,12 +214,13 @@
 
     def contract(s, tile, g, count):
         lines = rm[tile, s]
+        at_mix = tile * REACH * band
         for i in range(UNIT * count):
             line = jnp.broadcast_to(cw[tile, s, pl.ds(g * UNIT + i, 1), :], (band, 2 * cap))
-            mix[i * band : (i + 1) * band, :] = line.astype(jnp.bfloat16) * lines
+            mix[at_mix + i * band : at_mix + (i + 1) * band, :] = line.astype(jnp.bfloat16) * lines
         at = pl.multiple_of((tile * col_units + g) * unit, unit)
         acc[pl.ds(at, unit * count), :] += jnp.dot(
-            mix[pl.ds(0, unit * count), :],
+            mix[at_mix : at_mix + unit * count, :],
             x_in[tile, pl.ds(pl.multiple_of(2 * s * cap, 2 * cap), 2 * cap), :],
             preferred_element_type=jnp.float32,
         )
@@ -226,10 +229,11 @@
         count = span_units // over_units
 
         def one(i, none):
-            contract(s, i // count, i % count * over_units, over_units)
+            for tile in range(2):
+                contract(s, tile, i * over_units, over_units)
             return none
 
-        lax.fori_loop(0, 2 * count, one, 0)
+        lax.fori_loop(0, count, one, 0)
 
     take(last, (1 - mine,))
     add_step(last)
@@ -241,7 +245,6 @@
 
     lax.fori_loop(0, last - 1, middle_steps, 0)
     final = last - 1
-    take(final, (0, 1))
 
     def h_copy(side, u):
         return pltpu.make_async_remote_copy(
@@ -312,8 +315,9 @@
         at = pl.multiple_of(u * unit, unit)
         return acc[pl.ds(at, unit), :].astype(jnp.bfloat16).reshape(block)
 
-    for u in range(over_units):
-        for side in range(2):
+    for side in range(2):
+        take(final, (0, 1), (side,))
+        for u in range(over_units):
             g = u if side == 0 else col_units + over_units + u
             contract(final, side, g, 1)
             h_out[side, u] = rounded(side * col_units + g)
@@ -322,27 +326,30 @@
             def _(side=side, u=u):
                 h_copy(side, u).start()
 
+        if side == 0:
+            def rest(i, none):
+                contract(final, 0, (i + 1) * over_units, over_units)
+                return none
+
+            lax.fori_loop(0, span_units // over_units - 1, rest, 0)
+
     for m in range(spare):
         n = col_units + m - mine * spare
-        contract(final, 0, n + over_units, 1)
         contract(final, 1, n - spare, 1)
         y_out[m] = rounded(n + over_units)
         y_copy(m, m + mine * over_units).start()
 
     for m in range(spare):
         n = over_units + m + mine * spare
-        contract(final, 0, n + over_units, 1)
         contract(final, 1, n - spare, 1)
         t1[m + (1 - mine) * over_units, mine] = rounded(n + over_units)
         m_start(m + (1 - mine) * over_units, mine)
 
     ends = 2 * col_units - over_units
     for e in range(over_units):
-        contract(final, 0, e + over_units, 1)
         contract(final, 1, ends + e - spare, 1)
         if e >= spare:
             contract(final, 1, e - spare, 1)
-            contract(final, 0, ends + e + over_units, 1)
 
     totals = []
     for tile in range(2):
@@ -506,7 +513,7 @@
             pltpu.VMEM((pairs, 2, 2, 8, cap), f32),
             pltpu.VMEM((2, pairs, span, 2 * cap), f32),
             pltpu.VMEM((2, pairs, band, 2 * cap), bf16),
-            pltpu.VMEM((REACH * band, 2 * cap), bf16),
+            pltpu.VMEM((2 * REACH * band, 2 * cap), bf16),
             pltpu.VMEM((2 * (units + past) * unit, part), f32),
             pltpu.VMEM((2, past, UNIT, band, part), bf16),
             pltpu.VMEM((2, past, UNIT, band, part), bf16),

time: 59.9 us -> 60.7 us (1.013)
  no operation moved by 1% of the time
where the time goes in v6:
time: 60.7 us; the launch traced here: 59.9 us
  Pallas kernels  55.8 us (92%)
  other arithmetic  3.44 us (6%)
  between operations  0.65 us (1%)
    pallas_call x1, Pallas kernels, on_device(): pl.pallas_call(functools.partial(exchange_kernel, (n_dp, n_map, cap, cols...  55.8 us
    convert_element_type x1, other arithmetic, on_device(): return (updated, updated.astype(bf16))  3.44 us

profile of v6, /device:TPU:1, one launch (start us, length us, event | category | flops | bytes accessed | tf_op | source)
XLA Modules:
  0.0 59.9 jit_solution(18392405697873968497)
XLA Ops:
  0.6 0.0 copy-start
  0.6 55.8 %shard_map.50 = (bf16[32,64,256]{2,1,0:T(8,128)(2,1)}, f32[32,64]{1,0:T(8,128)}) custom-call(bf16[4096,256]{1,0:T(8,128)(2,1)} %emb_hbm.1, s32[1,4096]{1,0:T(1,128)} %bitcast.1), custom_call_target="tpu_custom_call" | custom-call | flops 8589934592 | bytes 3670016 | tf_op jit(solution)/shard_map/pallas_call | solution.py:498
  56.4 0.0 copy-done
  56.4 3.4 %fusion = (bf16[32,64,256]{2,1,0:T(8,128)(2,1)}, f32[32,64,256]{2,1,0:T(8,128)}) fusion(f32[32,64]{1,0:T(8,128)} %get-tuple-element.5, f32[32,64,256]{2,1,0:T(8,128)S(1)} %copy-done, bf16[32,64,256]{2,1,0:T(8,128)(2,1)} %get-tuple-element.4), kind=kLoop, calls=%fused_computation.1 | loop fusion | flops 3145728 | bytes 6299648 | tf_op jit(solution)/shard_map/convert_element_type | solution.py:543
Async XLA Ops:
  0.6 55.8 %copy-start = (f32[32,64,256]{2,1,0:T(8,128)S(1)}, f32[32,64,256]{2,1,0:T(8,128)}, u32[]{:S(2)}) copy-start(f32[32,64,256]{2,1,0:T(8,128)} %param.5) | copy-start | bytes 6291460

commit v7 on v5

--- a/solution.py
+++ b/solution.py
@@ -231,17 +231,14 @@
 
         lax.fori_loop(0, 2 * count, one, 0)
 
-    take(last, (1 - mine,))
-    add_step(last)
-
     def middle_steps(s, none):
         take(s, (0, 1))
         add_step(s)
         return none
 
-    lax.fori_loop(0, last - 1, middle_steps, 0)
-    final = last - 1
-    take(final, (0, 1))
+    lax.fori_loop(0, last, middle_steps, 0)
+    final = last
+    take(final, (1 - mine,))
 
     def h_copy(side, u):
         return pltpu.make_async_remote_copy(

time: 59.9 us -> 63.6 us (1.062)
  Pallas kernels: 55.2 us -> 58.9 us
    pallas_call x1, Pallas kernels: 55.2 us -> 58.9 us  [on_device(): pl.pallas_call(functools.partial(exchange_kernel, (n_dp, n_map, cap, cols...]
where the time goes in v7:
time: 63.6 us; the launch traced here: 63 us
  Pallas kernels  58.9 us (93%)
  other arithmetic  3.44 us (5%)
  between operations  0.65 us (1%)
    pallas_call x1, Pallas kernels, on_device(): pl.pallas_call(functools.partial(exchange_kernel, (n_dp, n_map, cap, cols...  58.9 us
    convert_element_type x1, other arithmetic, on_device(): return (updated, updated.astype(bf16))  3.44 us

profile of v7, /device:TPU:1, one launch (start us, length us, event | category | flops | bytes accessed | tf_op | source)
XLA Modules:
  0.0 63.0 jit_solution(5568187927849691471)
XLA Ops:
  0.6 0.0 copy-start
  0.6 58.9 %shard_map.50 = (bf16[32,64,256]{2,1,0:T(8,128)(2,1)}, f32[32,64]{1,0:T(8,128)}) custom-call(bf16[4096,256]{1,0:T(8,128)(2,1)} %emb_hbm.1, s32[1,4096]{1,0:T(1,128)} %bitcast.1), custom_call_target="tpu_custom_call" | custom-call | flops 8589934592 | bytes 3670016 | tf_op jit(solution)/shard_map/pallas_call | solution.py:488
  59.6 0.0 copy-done
  59.6 3.4 %fusion = (bf16[32,64,256]{2,1,0:T(8,128)(2,1)}, f32[32,64,256]{2,1,0:T(8,128)}) fusion(f32[32,64]{1,0:T(8,128)} %get-tuple-element.5, f32[32,64,256]{2,1,0:T(8,128)S(1)} %copy-done, bf16[32,64,256]{2,1,0:T(8,128)(2,1)} %get-tuple-element.4), kind=kLoop, calls=%fused_computation.1 | loop fusion | flops 3145728 | bytes 6299648 | tf_op jit(solution)/shard_map/convert_element_type | solution.py:533
Async XLA Ops:
  0.6 59.0 %copy-start = (f32[32,64,256]{2,1,0:T(8,128)S(1)}, f32[32,64,256]{2,1,0:T(8,128)}, u32[]{:S(2)}) copy-start(f32[32,64,256]{2,1,0:T(8,128)} %param.5) | copy-start | bytes 6291460
